TPU v7x, 32 devices: a whole 2x2x4 slice. The times are simulated.
32 devices in a mesh: tm: 2 (over core), rows: 16 (over z, y, x).
Axes of the slice: x: 2, y: 2, z: 4, core: 2. Of those that a mesh axis runs over, the one named last changes fastest.
Arguments:
- feat: bfloat16 [4, 32, 240, 512], P('tm', 'rows'), may hold values from -24 to 24
- norm1_gain: float32 [512], replicated, may hold values from 0.5 to 1.5
- norm1_bias: float32 [512], replicated, may hold values from -3 to 3
- conv_weight: bfloat16 [3, 3, 3, 512, 512], replicated, may hold values from -0.0546875 to 0.0546875
- conv_bias: float32 [512], replicated, may hold values from -3 to 3
- norm2_gain: float32 [512], replicated, may hold values from 0.5 to 1.5
- norm2_bias: float32 [512], replicated, may hold values from -3 to 3
- w_query: bfloat16 [512, 512], replicated, may hold values from -0.44194174 to 0.44194174
- w_key: bfloat16 [512, 512], replicated, may hold values from -1.5467961 to 1.5467961
- w_value: bfloat16 [512, 512], replicated, may hold values from -0.25 to 0.25
- w_out: bfloat16 [512, 512], replicated, may hold values from -0.25 to 0.25
- out_bias: float32 [512], replicated, may hold values from -3 to 3
Outputs:
- block_out: bfloat16 [4, 32, 240, 512], P('tm', 'rows')
All inputs are finite; a program needn't handle non-finite values.
Results may differ from a plain program's by a relative error of at most 0.0062.
The roundings to bfloat16 on the way count: a program that leaves them out, or rounds other values in their place, can miss the bound.
Values may be sent and summed in bfloat16 or wider, within the bound.
A program may use at most 128 MiB of HBM per device.

v0:
```python
import math

import jax
import jax.numpy as jnp
from jax import lax
from jax.sharding import PartitionSpec as P

GROUPS = 32
RADIUS = 4


EPS = 1e-06


def from_behind(array, axis, by):
    peers = lax.axis_size(axis)
    pairs = [(i, i + by) for i in range(peers) if 0 <= i + by < peers]
    return lax.ppermute(array, axis, pairs)


def padded_2(cells, sides, width):
    for axis, dim in sides:
        count = lax.axis_size(axis)
        ends = count - 1
        head = lax.slice_in_dim(cells, 0, width, axis=dim)
        tail = lax.slice_in_dim(cells, cells.shape[dim] - width, cells.shape[dim], axis=dim)
        cells = jnp.concatenate(
            [
                lax.ppermute(tail, axis, [(i, (i + 1) % count) for i in range(ends)]),
                cells,
                lax.ppermute(head, axis, [((i + 1) % count, i) for i in range(ends)]),
            ],
            axis=dim,
        )
    return cells


def group_norm(values, gain, shift, count):
    chans = values.shape[-1]
    grouped = values.reshape(values.shape[:-1] + (GROUPS, chans // GROUPS))
    local_sum = jnp.sum(grouped, axis=(0, 1, 2, 4))
    mean = lax.psum(local_sum, ("tm", "rows")) / count
    centered = grouped - mean[:, None]
    spread = lax.psum(jnp.sum(centered * centered, axis=(0, 1, 2, 4)), ("tm", "rows")) / count
    normed = centered * lax.rsqrt(spread + EPS)[:, None]
    return normed.reshape(values.shape) * gain + shift


def conv_taps(padded, weight, frames, height, width):
    chans = padded.shape[-1]
    total = jnp.zeros((frames * height * width, weight.shape[-1]), jnp.float32)
    for step_t in range(3):
        for step_h in range(3):
            slab = padded[step_t : step_t + frames, step_h : step_h + height]
            stacked = jnp.concatenate(
                [slab[:, :, step_w : step_w + width] for step_w in range(3)], axis=-1
            )
            total = total + jnp.dot(
                stacked.reshape(-1, 3 * chans),
                weight[step_t, step_h].reshape(3 * chans, -1),
                preferred_element_type=jnp.float32,
            )
    return total.reshape(frames, height, width, -1)


def project(flat, weight):
    return jnp.dot(flat, weight, preferred_element_type=jnp.float32).astype(jnp.bfloat16)


def shards(
    feat,
    norm1_gain,
    norm1_bias,
    conv_weight,
    conv_bias,
    norm2_gain,
    norm2_bias,
    w_query,
    w_key,
    w_value,
    w_out,
    out_bias,
):
    frames, stripe_rows, width, chans = feat.shape
    stripes = lax.axis_size("rows")
    count = lax.axis_size("tm") * stripes * frames * stripe_rows * width * (chans // GROUPS)
    act = jax.nn.silu(group_norm(feat.astype(jnp.float32), norm1_gain, norm1_bias, count)).astype(
        jnp.bfloat16
    )
    earlier = from_behind(act, "tm", 1)
    opening = jnp.broadcast_to(act[:1], earlier.shape)
    earlier = jnp.where(lax.axis_index("tm") == 0, opening, earlier)
    timed = jnp.concatenate([earlier, act], axis=0)
    rimmed = padded_2(timed, (("rows", 1),), 1)
    padded = jnp.pad(rimmed, ((0, 0), (0, 0), (1, 1), (0, 0)))
    conv = conv_taps(padded, conv_weight, frames, stripe_rows, width) + conv_bias
    resid = (feat.astype(jnp.float32) + conv).astype(jnp.bfloat16)
    normed = group_norm(resid.astype(jnp.float32), norm2_gain, norm2_bias, count).astype(
        jnp.bfloat16
    )
    flat = normed.reshape(-1, chans)
    query = project(flat, w_query).reshape(frames, -1, chans)
    reach = RADIUS * stripe_rows
    pieces = []
    for offset in range(-RADIUS, RADIUS + 1):
        if offset == 0:
            pieces.append(normed)
        else:
            pieces.append(from_behind(normed, "rows", -offset))
    wide = jnp.concatenate(pieces, axis=1)
    wide_flat = wide.reshape(-1, chans)
    keys = project(wide_flat, w_key).reshape(frames, -1, chans)
    values = project(wide_flat, w_value).reshape(frames, -1, chans)
    span = 2 * reach + stripe_rows
    place = lax.axis_index("rows") * stripe_rows - reach + jnp.arange(span, dtype=jnp.int32)
    valid = jnp.repeat((place >= 0) & (place < stripes * stripe_rows), width)
    scale = 1.0 / math.sqrt(chans)
    scores = jnp.einsum("fqc,fkc->fqk", query, keys, preferred_element_type=jnp.float32) * scale
    scores = jnp.where(valid[None, None, :], scores, jnp.float32(-1e30))
    top = jnp.max(scores, axis=-1, keepdims=True)
    expo = jnp.exp(scores - top)
    total = jnp.sum(expo, axis=-1, keepdims=True)
    mixed = jnp.einsum(
        "fqk,fkc->fqc", expo.astype(jnp.bfloat16), values, preferred_element_type=jnp.float32
    )
    attn = (mixed / total).astype(jnp.bfloat16).reshape(-1, chans)
    output = jnp.dot(attn, w_out, preferred_element_type=jnp.float32).reshape(
        frames, stripe_rows, width, chans
    )
    return (resid.astype(jnp.float32) + out_bias + output).astype(jnp.bfloat16)


def solution(mesh):
    return jax.shard_map(
        shards,
        mesh=mesh,
        in_specs=(
            P("tm", "rows", None, None),
            P(),
            P(),
            P(),
            P(),
            P(),
            P(),
            P(),
            P(),
            P(),
            P(),
            P(),
        ),
        out_specs=P("tm", "rows", None, None),
        check_vma=False,
    )
```

profile of v0, /device:TPU:4, one launch (start us, length us, event | category | flops | bytes accessed | tf_op | source)
XLA Modules:
  0.0 430.2 jit_solution(1380460038701066616)
XLA Ops:
  1.7 41.3 %psum.28 = f32[32]{0:T(128)S(1)} all-reduce(f32[32]{0:T(128)S(1)} %reduce_sum.59), channel_id=1, replica_groups=mesh['tm'=2,'rows'=16] {'tm','rows'}, use_global_device_ids=true, to_apply=%region_2.0 | all-reduce | flops 32 | bytes 256 | tf_op jit(solution)/shard_map/psum | solution.py:42
  44.9 40.2 %psum.29 = f32[32]{0:T(128)S(1)} all-reduce(f32[32]{0:T(128)S(1)} %reduce_sum.62), channel_id=1, replica_groups=mesh['tm'=2,'rows'=16] {'tm','rows'}, use_global_device_ids=true, to_apply=%region_5.6 | all-reduce | flops 32 | bytes 256 | tf_op jit(solution)/shard_map/psum | solution.py:44
  85.2 1.9 fusion.31
  88.5 2.1 collective-permute-done
  90.9 3.3 collective-permute-start.1
  94.2 3.6 collective-permute-start.2
  97.8 9.3 %fusion.43 = (bf16[1,1,3,512,512]{4,3,2,1,0:T(8,128)(2,1)S(1)}, bf16[1,1,3,512,512]{4,3,2,1,0:T(8,128)(2,1)}, bf16[1,1,3,512,512]{4,3,2,1,0:T(8,128)(2,1)}, bf16...) fusion(bf16[3,3,3,512,512]{4,3,2,1,0:T(8,128)(2,1)} %param.15), kind=kLoop, calls=%fused_computation.87 | loop fusion | bytes 28311552 | tf_op jit(solution)/shard_map/slice | solution.py:60
  107.1 11.1 %collective-permute-done.1 = bf16[4,1,240,512]{3,2,1,0:T(8,128)(2,1)S(1)} collective-permute-done((bf16[4,1,240,512]{3,2,1,0:T(8,128)(2,1)S(1)}, bf16[4,1,240,512]{3,2,1,0:T(8,128)(2,1)S(1)}, u32[]{:S(2)}, u32[]{:S(2)}) %collective-permute-start.1) | collective-permute-done | bytes 983072 | tf_op jit(solution)/shard_map/ppermute | solution.py:29
  118.2 18.5 %collective-permute-done.2 = bf16[4,1,240,512]{3,2,1,0:T(8,128)(2,1)S(1)} collective-permute-done((bf16[4,1,240,512]{3,2,1,0:T(8,128)(2,1)S(1)}, bf16[4,1,240,512]{3,2,1,0:T(8,128)(2,1)S(1)}, u32[]{:S(2)}, u32[]{:S(2)}) %collective-permute-start.2) | collective-permute-done | bytes 983072 | tf_op jit(solution)/shard_map/ppermute | solution.py:31
  136.8 2.1 select_maximum_fusion
  138.9 6.3 %fusion.44 = (bf16[2,2,240,512]{3,2,1,0:T(8,128)(2,1)S(1)}, bf16[2,2,240,512]{3,2,1,0:T(8,128)(2,1)S(1)}, bf16[2,2,240,512]{3,2,1,0:T(8,128)(2,1)S(1)}, bf16[2,2...) fusion(bf16[4,4,242,512]{3,2,1,0:T(8,128)(2,1)S(1)} %select_max, ...), kind=kLoop, calls=%fused_computation.88 | loop fusion | bytes 35389440 | tf_op jit(solution)/shard_map/slice | solution.py:56
  149.5 1.7 fusion.47
  154.7 1.7 fusion.50
  167.7 2.5 add_add_fusion
  170.9 41.0 %psum.30 = f32[32]{0:T(128)S(1)} all-reduce(f32[32]{0:T(128)S(1)} %reduce_sum.81), channel_id=1, replica_groups=mesh['tm'=2,'rows'=16] {'tm','rows'}, use_global_device_ids=true, to_apply=%region_8.9 | all-reduce | flops 32 | bytes 256 | tf_op jit(solution)/shard_map/psum | solution.py:42
  212.6 41.0 %psum.31 = f32[32]{0:T(128)S(1)} all-reduce(f32[32]{0:T(128)S(1)} %reduce_sum.84), channel_id=1, replica_groups=mesh['tm'=2,'rows'=16] {'tm','rows'}, use_global_device_ids=true, to_apply=%region_11.12 | all-reduce | flops 32 | bytes 256 | tf_op jit(solution)/shard_map/psum | solution.py:44
  254.2 3.4 collective-permute-start.3
  257.6 4.0 collective-permute-start.4
  261.6 1.9 collective-permute-start.5
  263.5 2.4 collective-permute-start.6
  266.1 4.3 %collective-permute-start.7 = (bf16[2,2,240,512]{3,2,1,0:T(8,128)(2,1)S(1)}, bf16[2,2,240,512]{3,2,1,0:T(8,128)(2,1)S(1)}, u32[]{:S(2)}, u32[]{:S(2)}) collective-permute-start(bf16[2,2,240,512]{3,2,1,0:T(8,128)(2,1)S(1)} %fusion.22), channel_id=1, source_target_pairs={{1,0},{2,1},{3,2},{4,3},{5,4},{6,5},{7,6},{8,7},{9,8},{10,9},{11,1... | collective-permute-start | bytes 2949128 | tf_op jit(solution)/shard_map/ppermute | solution.py:18
  270.5 8.3 %collective-permute-done.3 = bf16[2,2,240,512]{3,2,1,0:T(8,128)(2,1)} collective-permute-done((bf16[2,2,240,512]{3,2,1,0:T(8,128)(2,1)S(1)}, bf16[2,2,240,512]{3,2,1,0:T(8,128)(2,1)}, u32[]{:S(2)}, u32[]{:S(2)}) %collective-permute-start.3) | collective-permute-done | bytes 983072 | tf_op jit(solution)/shard_map/ppermute | solution.py:18
  278.8 1.9 collective-permute-start.8
  280.7 1.7 convolution_convert_fusion.2
  282.4 17.5 %collective-permute-done.4 = bf16[2,2,240,512]{3,2,1,0:T(8,128)(2,1)} collective-permute-done((bf16[2,2,240,512]{3,2,1,0:T(8,128)(2,1)S(1)}, bf16[2,2,240,512]{3,2,1,0:T(8,128)(2,1)}, u32[]{:S(2)}, u32[]{:S(2)}) %collective-permute-start.4) | collective-permute-done | bytes 983072 | tf_op jit(solution)/shard_map/ppermute | solution.py:18
  302.5 45.5 %collective-permute-done.5 = bf16[2,2,240,512]{3,2,1,0:T(8,128)(2,1)} collective-permute-done((bf16[2,2,240,512]{3,2,1,0:T(8,128)(2,1)S(1)}, bf16[2,2,240,512]{3,2,1,0:T(8,128)(2,1)}, u32[]{:S(2)}, u32[]{:S(2)}) %collective-permute-start.5) | collective-permute-done | bytes 983072 | tf_op jit(solution)/shard_map/ppermute | solution.py:18
  352.5 28.4 %collective-permute-done.10 = bf16[2,2,240,512]{3,2,1,0:T(8,128)(2,1)S(1)} collective-permute-done((bf16[2,2,240,512]{3,2,1,0:T(8,128)(2,1)S(1)}, bf16[2,2,240,512]{3,2,1,0:T(8,128)(2,1)S(1)}, u32[]{:S(2)}, u32[]{:S(2)}) %collective-permute-start.10) | collective-permute-done | bytes 983072 | tf_op jit(solution)/shard_map/ppermute | solution.py:18
  381.0 7.4 %convolution_convert_fusion.1 = bf16[8640,512]{1,0:T(8,128)(2,1)} fusion(bf16[8640,512]{1,0:T(8,128)(2,1)S(1)} %bitcast.80, bf16[512,512]{1,0:T(8,128)(2,1)S(1)} %copy-done), kind=kOutput, calls=%fused_computation.4 | convolution fusion | flops 4534272000 | bytes 18219008 | tf_op jit(solution)/shard_map/dot_general | solution.py:67
  388.4 7.2 %convolution_convert_fusion = bf16[8640,512]{1,0:T(8,128)(2,1)} fusion(bf16[8640,512]{1,0:T(8,128)(2,1)S(1)} %bitcast.81, bf16[512,512]{1,0:T(8,128)(2,1)S(1)} %copy-done.22), kind=kOutput, calls=%fused_computation.3 | convolution fusion | flops 4534272000 | bytes 18219008 | tf_op jit(solution)/shard_map/dot_general | solution.py:67
  395.6 12.3 %fusion = (f32[2,480]{1,0:T(2,128)S(1)}, f32[2,480,4320]{2,1,0:T(8,128)}) fusion(pred[4320]{0:T(1024)(128)(4,1)S(1)} %broadcast_in_dim.35, bf16[2,480,512]{2,1,0:T(8,128)(2,1)S(1)} %bitcast.84, bf16[2,4320,512]{2,1,0:T(8,128)(2,1)} %bitcast.83), kind=kOutput, calls=%fused_computation.2 | convolution fusion | flops 4259173376 | bytes 26427360 | tf_op jit(solution)/shard_map/fqc,fkc->fqk/dot_general | solution.py:118
  407.9 9.5 %fusion.1 = f32[2,480]{1,0:T(2,128)S(1)} fusion(f32[2,480,4320]{2,1,0:T(8,128)} %get-tuple-element.48, f32[2,480]{1,0:T(2,128)S(1)} %get-tuple-element.47, pred[4320]{0:T(1024)(128)(4,1)S(1)} %broadcast_in_dim.35), kind=kLoop, calls=%fused_computation.5 | loop fusion | flops 16587840 | bytes 16600800 | tf_op jit(solution)/shard_map/reduce_sum | solution.py:122
  417.4 11.2 %divide_convert_fusion = bf16[2,480,512]{2,1,0:T(8,128)(2,1)S(1)} fusion(bf16[2,4320,512]{2,1,0:T(8,128)(2,1)} %bitcast.82, f32[2,480,4320]{2,1,0:T(8,128)} %get-tuple-element.48, f32[2,480]{1,0:T(2,128)S(1)} %get-tuple-element.47, pred[4320]{0:T(1024)(128)(4,1)S(1)} %broadcast_in_dim.35, f32[2,480]{1,0:T(2,128)S(1)} %fusion.1), kind=kOutput, calls=%fused_computation.63 | convolution fusion | flops 4264304640 | bytes 26431200 | tf_op jit(solution)/shard_map/fqk,fkc->fqc/dot_general | solution.py:123
  (111 shorter events, 35.1 us)
Async XLA Ops:
  0.0 381.0 %copy-start = (bf16[512,512]{1,0:T(8,128)(2,1)S(1)}, bf16[512,512]{1,0:T(8,128)(2,1)}, u32[]{:S(2)}) copy-start(bf16[512,512]{1,0:T(8,128)(2,1)} %param.20) | copy-start | bytes 1572868
  87.1 3.5 collective-permute-start
  90.9 27.4 %collective-permute-start.1 = (bf16[4,1,240,512]{3,2,1,0:T(8,128)(2,1)S(1)}, bf16[4,1,240,512]{3,2,1,0:T(8,128)(2,1)S(1)}, u32[]{:S(2)}, u32[]{:S(2)}) collective-permute-start(bf16[4,1,240,512]{3,2,1,0:T(8,128)(2,1)S(1)} %get-tuple-element.42), channel_id=1, source_target_pairs={{0,1},{1,2},{2,3},{3,4},{4,5},{5,6},{6,7},{7,8},{8,9},{9,10},{10,1... | collective-permute-start | bytes 2949128 | tf_op jit(solution)/shard_map/ppermute | solution.py:29
  94.2 42.6 %collective-permute-start.2 = (bf16[4,1,240,512]{3,2,1,0:T(8,128)(2,1)S(1)}, bf16[4,1,240,512]{3,2,1,0:T(8,128)(2,1)S(1)}, u32[]{:S(2)}, u32[]{:S(2)}) collective-permute-start(bf16[4,1,240,512]{3,2,1,0:T(8,128)(2,1)S(1)} %get-tuple-element.43), channel_id=1, source_target_pairs={{1,0},{2,1},{3,2},{4,3},{5,4},{6,5},{7,6},{8,7},{9,8},{10,9},{11,1... | collective-permute-start | bytes 2949128 | tf_op jit(solution)/shard_map/ppermute | solution.py:31
  146.0 1.5 copy-start.8
  146.0 1.8 copy-start.9
  146.0 2.1 copy-start.10
  149.5 1.7 copy-start.17
  151.2 1.7 copy-start.3
  151.2 1.7 copy-start.4
  151.2 1.8 copy-start.5
  151.2 2.1 copy-start.6
  154.7 1.7 copy-start.15
  156.4 1.7 copy-start.2
  161.2 1.4 copy-start.13
  162.6 1.7 copy-start.12
  164.3 1.7 copy-start.11
  167.7 2.5 copy-start.1
  167.7 2.5 copy-start.21
  170.2 83.6 %copy-start.19 = (f32[512]{0:T(512)S(1)}, f32[512]{0:T(512)}, u32[]{:S(2)}) copy-start(f32[512]{0:T(512)} %param.18) | copy-start | bytes 6148
  170.2 83.5 %copy-start.20 = (f32[512]{0:T(512)S(1)}, f32[512]{0:T(512)}, u32[]{:S(2)}) copy-start(f32[512]{0:T(512)} %param.17) | copy-start | bytes 6148
  254.2 24.6 %collective-permute-start.3 = (bf16[2,2,240,512]{3,2,1,0:T(8,128)(2,1)S(1)}, bf16[2,2,240,512]{3,2,1,0:T(8,128)(2,1)}, u32[]{:S(2)}, u32[]{:S(2)}) collective-permute-start(bf16[2,2,240,512]{3,2,1,0:T(8,128)(2,1)S(1)} %fusion.22), channel_id=1, source_target_pairs={{0,4},{1,5},{2,6},{3,7},{4,8},{5,9},{6,10},{7,11},{8,12},{9,13},{1... | collective-permute-start | bytes 2949128 | tf_op jit(solution)/shard_map/ppermute | solution.py:18
  257.6 42.4 %collective-permute-start.4 = (bf16[2,2,240,512]{3,2,1,0:T(8,128)(2,1)S(1)}, bf16[2,2,240,512]{3,2,1,0:T(8,128)(2,1)}, u32[]{:S(2)}, u32[]{:S(2)}) collective-permute-start(bf16[2,2,240,512]{3,2,1,0:T(8,128)(2,1)S(1)} %fusion.22), channel_id=1, source_target_pairs={{0,3},{1,4},{2,5},{3,6},{4,7},{5,8},{6,9},{7,10},{8,11},{9,12},{10... | collective-permute-start | bytes 2949128 | tf_op jit(solution)/shard_map/ppermute | solution.py:18
  261.6 86.4 %collective-permute-start.5 = (bf16[2,2,240,512]{3,2,1,0:T(8,128)(2,1)S(1)}, bf16[2,2,240,512]{3,2,1,0:T(8,128)(2,1)}, u32[]{:S(2)}, u32[]{:S(2)}) collective-permute-start(bf16[2,2,240,512]{3,2,1,0:T(8,128)(2,1)S(1)} %fusion.22), channel_id=1, source_target_pairs={{0,2},{1,3},{2,4},{3,5},{4,6},{5,7},{6,8},{7,9},{8,10},{9,11},{10,... | collective-permute-start | bytes 2949128 | tf_op jit(solution)/shard_map/ppermute | solution.py:18
  263.5 88.3 %collective-permute-start.6 = (bf16[2,2,240,512]{3,2,1,0:T(8,128)(2,1)S(1)}, bf16[2,2,240,512]{3,2,1,0:T(8,128)(2,1)S(1)}, u32[]{:S(2)}, u32[]{:S(2)}) collective-permute-start(bf16[2,2,240,512]{3,2,1,0:T(8,128)(2,1)S(1)} %fusion.22), channel_id=1, source_target_pairs={{0,1},{1,2},{2,3},{3,4},{4,5},{5,6},{6,7},{7,8},{8,9},{9,10},{10,1... | collective-permute-start | bytes 2949128 | tf_op jit(solution)/shard_map/ppermute | solution.py:18
  266.1 86.1 %collective-permute-start.7 = (bf16[2,2,240,512]{3,2,1,0:T(8,128)(2,1)S(1)}, bf16[2,2,240,512]{3,2,1,0:T(8,128)(2,1)S(1)}, u32[]{:S(2)}, u32[]{:S(2)}) collective-permute-start(bf16[2,2,240,512]{3,2,1,0:T(8,128)(2,1)S(1)} %fusion.22), channel_id=1, source_target_pairs={{1,0},{2,1},{3,2},{4,3},{5,4},{6,5},{7,6},{8,7},{9,8},{10,9},{11,1... | collective-permute-start | bytes 2949128 | tf_op jit(solution)/shard_map/ppermute | solution.py:18
  278.8 73.5 %collective-permute-start.8 = (bf16[2,2,240,512]{3,2,1,0:T(8,128)(2,1)S(1)}, bf16[2,2,240,512]{3,2,1,0:T(8,128)(2,1)S(1)}, u32[]{:S(2)}, u32[]{:S(2)}) collective-permute-start(bf16[2,2,240,512]{3,2,1,0:T(8,128)(2,1)S(1)} %fusion.22), channel_id=1, source_target_pairs={{2,0},{3,1},{4,2},{5,3},{6,4},{7,5},{8,6},{9,7},{10,8},{11,9},{12,... | collective-permute-start | bytes 2949128 | tf_op jit(solution)/shard_map/ppermute | solution.py:18
  299.9 52.5 %collective-permute-start.9 = (bf16[2,2,240,512]{3,2,1,0:T(8,128)(2,1)S(1)}, bf16[2,2,240,512]{3,2,1,0:T(8,128)(2,1)S(1)}, u32[]{:S(2)}, u32[]{:S(2)}) collective-permute-start(bf16[2,2,240,512]{3,2,1,0:T(8,128)(2,1)S(1)} %fusion.22), channel_id=1, source_target_pairs={{3,0},{4,1},{5,2},{6,3},{7,4},{8,5},{9,6},{10,7},{11,8},{12,9},{13... | collective-permute-start | bytes 2949128 | tf_op jit(solution)/shard_map/ppermute | solution.py:18
  348.0 33.0 %collective-permute-start.10 = (bf16[2,2,240,512]{3,2,1,0:T(8,128)(2,1)S(1)}, bf16[2,2,240,512]{3,2,1,0:T(8,128)(2,1)S(1)}, u32[]{:S(2)}, u32[]{:S(2)}) collective-permute-start(bf16[2,2,240,512]{3,2,1,0:T(8,128)(2,1)S(1)} %fusion.22), channel_id=1, source_target_pairs={{4,0},{5,1},{6,2},{7,3},{8,4},{9,5},{10,6},{11,7},{12,8},{13,9},{1... | collective-permute-start | bytes 2949128 | tf_op jit(solution)/shard_map/ppermute | solution.py:18
  381.0 7.4 %copy-start.22 = (bf16[512,512]{1,0:T(8,128)(2,1)S(1)}, bf16[512,512]{1,0:T(8,128)(2,1)}, u32[]{:S(2)}) copy-start(bf16[512,512]{1,0:T(8,128)(2,1)} %param.21) | copy-start | bytes 1572868
  417.3 11.2 %copy-start.23 = (bf16[512,512]{1,0:T(8,128)(2,1)S(1)}, bf16[512,512]{1,0:T(8,128)(2,1)}, u32[]{:S(2)}) copy-start(bf16[512,512]{1,0:T(8,128)(2,1)} %param.22) | copy-start | bytes 1572868
  417.4 11.2 %copy-start.24 = (f32[512]{0:T(512)S(1)}, f32[512]{0:T(512)}, u32[]{:S(2)}) copy-start(f32[512]{0:T(512)} %param.23) | copy-start | bytes 6148
  (4 other events, 5.4 us)
where the time goes:
time: 431 us; the launch traced here: 430 us
  blocking collectives  164 us (38%)
  waiting for transfers between devices  131 us (30%)
  matrix products  57.3 us (13%)
  starting transfers between devices  28.8 us (7%)
  local copies, waits for them, and re-layouts  26.9 us (6%)
  other arithmetic  21.6 us (5%)
    ppermute x9, waiting for transfers between devices, from_behind(): return lax.ppermute(array, axis, pairs)  102 us
    psum x2, blocking collectives, group_norm(): mean = lax.psum(local_sum, ('tm', 'rows')) / count  82.3 us
    psum x2, blocking collectives, group_norm(): lax.psum(jnp.sum(centered * centered, axis=(0, 1, 2, 4)), ('tm', 'rows'))  81.2 us
    ppermute x9, starting transfers between devices, from_behind(): return lax.ppermute(array, axis, pairs)  21.9 us
    ppermute x1, waiting for transfers between devices, padded_2(): lax.ppermute(head, axis, [((i + 1) % count, i) for i in range(ends)])  18.5 us
    dot_general x3, matrix products, project(): jnp.dot(flat, weight, preferred_element_type=jnp.float32)  16.3 us
    dot_general x9, matrix products, conv_taps(): jnp.dot(stacked.reshape(-1, 3 * chans), weight[step_t, step_h].reshape(3...  15.9 us
    dot_general x1, matrix products, shards(): jnp.einsum('fqc,fkc->fqk', query, keys, preferred_element_type=jnp.float32)  12.3 us
  transfers between devices with their start and end apart: 11, of which 7 were waited for; matrix products, arithmetic and copies ran while one was open for 4% of the time, Pallas kernels for 0%

commit v1 on v0

v1 whole, which is shorter than its diff:
```python
import functools
import math

import jax
import jax.numpy as jnp
from jax import lax
from jax.experimental import pallas as pl
from jax.experimental.pallas import tpu as pltpu
from jax.sharding import PartitionSpec as P

GROUPS = 32
EPS = 1e-06
BAND = 4
MESH = pl.DeviceIdType.MESH
VMEM_LIMIT = 56 * 1024 * 1024


def greet_all(count, stripes, me):
    barrier = pltpu.get_barrier_semaphore()

    def greet(step, carry):
        peer = (me + step) % count
        pl.semaphore_signal(
            barrier, inc=1, device_id=(peer // stripes, peer % stripes), device_id_type=MESH
        )
        return carry

    lax.fori_loop(1, count, greet, 0)
    pl.semaphore_wait(barrier, count - 1)


def send_stats(count, stripes, me, stat_ref, all_ref, send_sem, recv_sem):
    all_ref[me] = stat_ref[0]

    def send(step, carry):
        peer = (me + step) % count
        pltpu.make_async_remote_copy(
            src_ref=stat_ref.at[0],
            dst_ref=all_ref.at[me],
            send_sem=send_sem,
            recv_sem=recv_sem,
            device_id=(peer // stripes, peer % stripes),
            device_id_type=MESH,
        ).start()
        return carry

    lax.fori_loop(1, count, send, 0)


def wait_stats(count, all_ref, send_sem, recv_sem):
    others = all_ref.at[pl.ds(0, count - 1)]
    pltpu.make_async_copy(others, others, recv_sem).wait()
    pltpu.make_async_copy(others, others, send_sem).wait()


def stats_kernel(sections, stripes, stat_ref, all_ref, send_sem, recv_sem):
    count = sections * stripes
    me = lax.axis_index("tm") * stripes + lax.axis_index("rows")
    greet_all(count, stripes, me)
    send_stats(count, stripes, me, stat_ref, all_ref, send_sem, recv_sem)
    wait_stats(count, all_ref, send_sem, recv_sem)


def halo_kernel(
    sections,
    stripes,
    stat_ref,
    feat_ref,
    all_ref,
    ext_ref,
    send_sem,
    recv_sem,
    local_sem,
    out_sem,
    in_sem,
):
    count = sections * stripes
    tm = lax.axis_index("tm")
    row = lax.axis_index("rows")
    me = tm * stripes + row
    frames, high = feat_ref.shape[:2]
    own = pltpu.make_async_copy(
        feat_ref, ext_ref.at[pl.ds(frames, frames), pl.ds(1, high)], local_sem
    )
    own.start()
    greet_all(count, stripes, me)
    send_stats(count, stripes, me, stat_ref, all_ref, send_sem, recv_sem)

    def push(src, dst, slot, to_tm, to_row):
        return pltpu.make_async_remote_copy(
            src_ref=src,
            dst_ref=dst,
            send_sem=out_sem.at[slot],
            recv_sem=in_sem.at[slot],
            device_id=(to_tm, to_row),
            device_id_type=MESH,
        )

    now = pl.ds(frames, frames)
    past = pl.ds(0, frames)
    down = push(feat_ref.at[:, high - 1], ext_ref.at[now, 0], 0, tm, row + 1)
    up = push(feat_ref.at[:, 0], ext_ref.at[now, high + 1], 1, tm, row - 1)
    later = push(feat_ref, ext_ref.at[past, pl.ds(1, high)], 2, tm + 1, row)
    later_top = push(ext_ref.at[now, 0], ext_ref.at[past, 0], 3, tm + 1, row)
    later_low = push(ext_ref.at[now, high + 1], ext_ref.at[past, high + 1], 4, tm + 1, row)
    has_next = tm < sections - 1
    has_past = tm > 0
    has_above = row > 0
    has_below = row < stripes - 1

    pl.when(has_below)(lambda: down.start())
    pl.when(has_above)(lambda: up.start())
    pl.when(has_next)(lambda: later.start())

    @pl.when(has_above)
    def _():
        down.wait_recv()
        pl.when(has_next)(lambda: later_top.start())

    @pl.when(has_below)
    def _():
        up.wait_recv()
        pl.when(has_next)(lambda: later_low.start())

    @pl.when(has_past)
    def _():
        later.wait_recv()
        pl.when(has_above)(lambda: later_top.wait_recv())
        pl.when(has_below)(lambda: later_low.wait_recv())

    pl.when(has_below)(lambda: down.wait_send())
    pl.when(has_above)(lambda: up.wait_send())

    @pl.when(has_next)
    def _():
        later.wait_send()
        pl.when(has_above)(lambda: later_top.wait_send())
        pl.when(has_below)(lambda: later_low.wait_send())

    own.wait()
    wait_stats(count, all_ref, send_sem, recv_sem)


def attend_kernel(
    stripes,
    normed_ref,
    wq_ref,
    wk_ref,
    wv_ref,
    out_ref,
    window,
    query,
    key,
    value,
    top,
    total,
    mixed,
    reply,
    in_sem,
    out_sem,
    back_in,
    back_out,
):
    bands = stripes // BAND
    tm = lax.axis_index("tm")
    row = lax.axis_index("rows")
    band = row // BAND
    k = row % BAND
    first = band * BAND
    cells, chans = normed_ref.shape[1:]
    scale = 1.0 / math.sqrt(chans)
    has_above = band > 0
    has_below = band < bands - 1
    half = k // 2

    barrier = pltpu.get_barrier_semaphore()

    def greet(to_tm, to_row):
        pl.semaphore_signal(barrier, inc=1, device_id=(to_tm, to_row), device_id_type=MESH)

    greet(1 - tm, row)
    pl.when(has_above)(lambda: greet(tm, row - BAND))
    pl.when(has_below)(lambda: greet(tm, row + BAND))
    for j in range(2):
        pl.when(2 * tm + j != k)(lambda j=j: greet(half, first + 2 * tm + j))
    peers = 1 + has_above.astype(jnp.int32) + has_below.astype(jnp.int32)
    for j in range(2):
        peers = peers + (2 * tm + j != k).astype(jnp.int32)
    pl.semaphore_wait(barrier, peers)

    def push(src, dst, sent, got, to_tm, to_row):
        return pltpu.make_async_remote_copy(
            src_ref=src,
            dst_ref=dst,
            send_sem=sent,
            recv_sem=got,
            device_id=(to_tm, to_row),
            device_id_type=MESH,
        )

    def scatter(j):
        return push(
            normed_ref.at[j],
            window.at[BAND + k],
            out_sem.at[j],
            in_sem.at[BAND + k],
            half,
            first + 2 * tm + j,
        )

    for j in range(2):
        pl.when(2 * tm + j != k)(lambda j=j: scatter(j).start())

        @pl.when(2 * tm + j == k)
        def _(j=j):
            pltpu.make_async_copy(
                normed_ref.at[j], window.at[BAND + k], in_sem.at[BAND + k]
            ).start()

    def arrived(slot):
        pltpu.make_async_copy(window.at[slot], window.at[slot], in_sem.at[slot]).wait()

    def across(slot, number):
        return push(
            window.at[slot],
            window.at[slot],
            out_sem.at[number],
            in_sem.at[slot],
            1 - tm,
            row,
        )

    def downward(slot, number):
        return push(
            window.at[slot],
            window.at[slot - BAND],
            out_sem.at[number],
            in_sem.at[slot - BAND],
            tm,
            row + BAND,
        )

    def upward(slot, number):
        return push(
            window.at[slot],
            window.at[slot + BAND],
            out_sem.at[number],
            in_sem.at[slot + BAND],
            tm,
            row - BAND,
        )

    def update(q, slot):
        scores = (
            lax.dot_general(
                query[q], key[...], (((1,), (1,)), ((), ())), preferred_element_type=jnp.float32
            )
            * scale
        )
        old = top[q]
        new = jnp.maximum(old, jnp.max(scores, axis=-1, keepdims=True))
        expo = jnp.exp(scores - new[:, :1])
        shrink = jnp.exp(old - new)
        total[q] = total[q] * shrink + jnp.sum(expo, axis=-1, keepdims=True)
        top[q] = new
        mixed[q] = mixed[q] * shrink[:, :1] + jnp.dot(
            expo.astype(jnp.bfloat16), value[...], preferred_element_type=jnp.float32
        )

    def queries(t, carry):
        slot = BAND + 2 * tm + t
        arrived(slot)
        pl.when(has_below)(lambda: downward(slot, 2 + t).start())
        pl.when(has_above)(lambda: upward(slot, 4 + t).start())
        across(slot, 6 + t).start()
        query[t] = jnp.dot(window[slot], wq_ref[...], preferred_element_type=jnp.float32).astype(
            jnp.bfloat16
        )
        top[t] = jnp.full_like(top[t], -1e30)
        total[t] = jnp.zeros_like(total[t])
        mixed[t] = jnp.zeros_like(mixed[t])
        return carry

    lax.fori_loop(0, 2, queries, 0)

    def slots(t, carry):
        stage = t // 2
        i = t % 2
        slot = i + jnp.where(
            stage == 0,
            BAND + 2 * tm,
            jnp.where(
                stage == 1,
                BAND + 2 * (1 - tm),
                jnp.where(stage == 2, 2 * tm, jnp.where(stage == 3, 2 * BAND + 2 * tm, 2 + 6 * tm)),
            ),
        )
        inside = ((slot >= BAND) | has_above) & ((slot < 2 * BAND) | has_below)

        @pl.when(inside)
        def _():
            pl.when(stage > 0)(lambda: arrived(slot))
            pl.when((stage == 2) & (tm == 1))(lambda: across(slot, 8 + i).start())
            pl.when((stage == 3) & (tm == 0))(lambda: across(slot, 8 + i).start())
            key[...] = jnp.dot(
                window[slot], wk_ref[...], preferred_element_type=jnp.float32
            ).astype(jnp.bfloat16)
            value[...] = jnp.dot(
                window[slot], wv_ref[...], preferred_element_type=jnp.float32
            ).astype(jnp.bfloat16)

            def one(q, inner):
                start = 2 * tm + q
                pl.when((slot >= start) & (slot <= start + 2 * BAND))(lambda: update(q, slot))
                return inner

            lax.fori_loop(0, 2, one, 0)

        return carry

    lax.fori_loop(0, 10, slots, 0)

    def answer(q):
        return push(
            reply.at[q], out_ref.at[k % 2], back_out.at[q], back_in.at[k % 2], half, first + 2 * tm + q
        )

    for q in range(2):
        reply[q] = (mixed[q] / total[q][:, :1]).astype(jnp.bfloat16)
        pl.when(2 * tm + q != k)(lambda q=q: answer(q).start())

        @pl.when(2 * tm + q == k)
        def _(q=q):
            pltpu.make_async_copy(reply.at[q], out_ref.at[k % 2], back_in.at[k % 2]).start()

    for j in range(2):
        pltpu.make_async_copy(out_ref.at[j], out_ref.at[j], back_in.at[j]).wait()

        @pl.when(2 * tm + j != k)
        def _(j=j):
            scatter(j).wait_send()
            answer(j).wait_send()

        across(BAND + 2 * tm + j, 6 + j).wait_send()
        pl.when(has_below)(lambda j=j: downward(BAND + 2 * tm + j, 2 + j).wait_send())
        pl.when(has_above)(lambda j=j: upward(BAND + 2 * tm + j, 4 + j).wait_send())
        pl.when((tm == 1) & has_above)(lambda j=j: across(2 + j, 8 + j).wait_send())
        pl.when((tm == 0) & has_below)(lambda j=j: across(2 * BAND + j, 8 + j).wait_send())


def local_stats(values):
    chans = values.shape[-1]
    grouped = values.reshape(-1, GROUPS, chans // GROUPS)
    size = grouped.shape[0] * grouped.shape[2]
    mean = jnp.sum(grouped, axis=(0, 2)) / size
    centered = grouped - mean[:, None]
    spread = jnp.sum(centered * centered, axis=(0, 2))
    packed = jnp.concatenate([mean, spread, jnp.zeros((128 - 2 * GROUPS,), jnp.float32)])
    return packed.reshape(1, 1, 128), size


def norm_terms(stats, size, gain, shift):
    means = stats[:, 0, :GROUPS]
    spreads = stats[:, 0, GROUPS : 2 * GROUPS]
    mean = jnp.mean(means, axis=0)
    gap = means - mean
    spread = jnp.sum(spreads + size * gap * gap, axis=0) / (size * stats.shape[0])
    each = gain.shape[0] // GROUPS
    return jnp.repeat(mean, each), jnp.repeat(lax.rsqrt(spread + EPS), each) * gain, shift


def normalize(values, terms):
    mean, gain, shift = terms
    return (values - mean) * gain + shift


def conv_taps(padded, weight, frames, height, width):
    chans = padded.shape[-1]
    total = jnp.zeros((frames * height * width, weight.shape[-1]), jnp.float32)
    for step_t in range(3):
        for step_h in range(3):
            slab = padded[step_t : step_t + frames, step_h : step_h + height]
            stacked = jnp.concatenate(
                [slab[:, :, step_w : step_w + width] for step_w in range(3)], axis=-1
            )
            total = total + jnp.dot(
                stacked.reshape(-1, 3 * chans),
                weight[step_t, step_h].reshape(3 * chans, -1),
                preferred_element_type=jnp.float32,
            )
    return total.reshape(frames, height, width, -1)


def shards(
    feat,
    norm1_gain,
    norm1_bias,
    conv_weight,
    conv_bias,
    norm2_gain,
    norm2_bias,
    w_query,
    w_key,
    w_value,
    w_out,
    out_bias,
):
    frames, high, width, chans = feat.shape
    sections = lax.axis_size("tm")
    stripes = lax.axis_size("rows")
    count = sections * stripes
    row = lax.axis_index("rows")
    vmem = pl.BlockSpec(memory_space=pltpu.VMEM)
    anywhere = pl.BlockSpec(memory_space=pl.ANY)
    all_stats = jax.ShapeDtypeStruct((count, 1, 128), jnp.float32)
    dma = pltpu.SemaphoreType.DMA

    stat1, size = local_stats(feat.astype(jnp.float32))
    stats1, ext = pl.pallas_call(
        functools.partial(halo_kernel, sections, stripes),
        out_shape=(
            all_stats,
            jax.ShapeDtypeStruct((2 * frames, high + 2, width, chans), jnp.bfloat16),
        ),
        in_specs=[vmem, anywhere],
        out_specs=(vmem, anywhere),
        scratch_shapes=[dma, dma, dma, dma((5,)), dma((5,))],
        compiler_params=pltpu.CompilerParams(collective_id=0, has_side_effects=True),
        name="halo",
    )(stat1, feat)
    act = jax.nn.silu(
        normalize(ext.astype(jnp.float32), norm_terms(stats1, size, norm1_gain, norm1_bias))
    ).astype(jnp.bfloat16)
    opening = jnp.broadcast_to(act[frames : frames + 1], act[:frames].shape)
    past = jnp.where(lax.axis_index("tm") == 0, opening, act[:frames])
    timed = jnp.concatenate([past, act[frames:]], axis=0)
    place = row * high - 1 + jnp.arange(high + 2, dtype=jnp.int32)
    within = (place >= 0) & (place < stripes * high)
    timed = jnp.where(within[None, :, None, None], timed, jnp.bfloat16(0))
    padded = jnp.pad(timed, ((0, 0), (0, 0), (1, 1), (0, 0)))
    conv = conv_taps(padded, conv_weight, frames, high, width) + conv_bias
    resid = (feat.astype(jnp.float32) + conv).astype(jnp.bfloat16)

    stat2, size = local_stats(resid.astype(jnp.float32))
    stats2 = pl.pallas_call(
        functools.partial(stats_kernel, sections, stripes),
        out_shape=all_stats,
        in_specs=[vmem],
        out_specs=vmem,
        scratch_shapes=[dma, dma],
        compiler_params=pltpu.CompilerParams(collective_id=1, has_side_effects=True),
        name="stats",
    )(stat2)
    normed = normalize(
        resid.astype(jnp.float32), norm_terms(stats2, size, norm2_gain, norm2_bias)
    ).astype(jnp.bfloat16)
    cells = high * width
    attn = pl.pallas_call(
        functools.partial(attend_kernel, stripes),
        out_shape=jax.ShapeDtypeStruct((frames, cells, chans), jnp.bfloat16),
        in_specs=[vmem] * 4,
        out_specs=vmem,
        scratch_shapes=[
            pltpu.VMEM((3 * BAND, cells, chans), jnp.bfloat16),
            pltpu.VMEM((2, cells, chans), jnp.bfloat16),
            pltpu.VMEM((cells, chans), jnp.bfloat16),
            pltpu.VMEM((cells, chans), jnp.bfloat16),
            pltpu.VMEM((2, cells, 128), jnp.float32),
            pltpu.VMEM((2, cells, 128), jnp.float32),
            pltpu.VMEM((2, cells, chans), jnp.float32),
            pltpu.VMEM((2, cells, chans), jnp.bfloat16),
            dma((3 * BAND,)),
            dma((10,)),
            dma((2,)),
            dma((2,)),
        ],
        compiler_params=pltpu.CompilerParams(
            collective_id=2, has_side_effects=True, vmem_limit_bytes=VMEM_LIMIT
        ),
        name="attend",
    )(normed.reshape(frames, cells, chans), w_query, w_key, w_value)
    output = jnp.dot(
        attn.reshape(-1, chans), w_out, preferred_element_type=jnp.float32
    ).reshape(frames, high, width, chans)
    return (resid.astype(jnp.float32) + out_bias + output).astype(jnp.bfloat16)


def solution(mesh):
    return jax.shard_map(
        shards,
        mesh=mesh,
        in_specs=(
            P("tm", "rows", None, None),
            P(),
            P(),
            P(),
            P(),
            P(),
            P(),
            P(),
            P(),
            P(),
            P(),
            P(),
        ),
        out_specs=P("tm", "rows", None, None),
        check_vma=False,
    )
```

time: 431 us -> 182 us (0.42)
  the two profiles are of different devices: /device:TPU:4 before, /device:TPU:9 now
where the time goes in v1:
time: 182 us; the launch traced here: 179 us
  Pallas kernels  106 us (58%)
  other arithmetic  26.5 us (15%)
  local copies, waits for them, and re-layouts  25.5 us (14%)
  matrix products  20.8 us (11%)
    pallas_call x1, Pallas kernels, shards(): pl.pallas_call(functools.partial(attend_kernel, stripes), out_shape=jax.S...  64.8 us
    pallas_call x1, Pallas kernels, shards(): pl.pallas_call(functools.partial(halo_kernel, sections, stripes), out_sha...  32.2 us
    dot_general x9, matrix products, conv_taps(): jnp.dot(stacked.reshape(-1, 3 * chans), weight[step_t, step_h].reshape(3...  18 us
    slice x3, local copies, waits for them, and re-layouts, conv_taps(): slab[:, :, step_w:step_w + width]  11.7 us
    pallas_call x1, Pallas kernels, shards(): pl.pallas_call(functools.partial(stats_kernel, sections, stripes), out_sh...  8.82 us
    concatenate x5, other arithmetic, conv_taps(): jnp.concatenate([slab[:, :, step_w:step_w + width] for step_w in range(3)...  7.15 us
    unnamed x48, local copies, waits for them, and re-layouts  6.43 us
    slice x1, local copies, waits for them, and re-layouts, conv_taps(): weight[step_t, step_h].reshape(3 * chans, -1)  5.3 us

profile of v1, /device:TPU:9, one launch (start us, length us, event | category | flops | bytes accessed | tf_op | source)
XLA Modules:
  0.0 179.2 jit_solution(9695527800078731618)
XLA Ops:
  0.0 1.5 convert_reduce_fusion.1
  1.8 1.5 fusion.1
  4.2 32.2 %halo.1 = (f32[32,1,128]{2,1,0:T(1,128)}, bf16[4,4,240,512]{3,2,1,0:T(8,128)(2,1)}) custom-call(f32[1,1,128]{2,1,0:T(1,128)} %fusion.15.stat_ref, bf16[2,2,240,512]{3,2,1,0:T(8,128)(2,1)} %feat_ref.1), custom_call_target="tpu_custom_call" | custom-call | tf_op jit(solution)/shard_map/halo/pallas_call | solution.py:419
  37.2 0.9 fusion.12
  38.4 4.0 %multiply_convert_fusion = bf16[4,4,240,512]{3,2,1,0:T(8,128)(2,1)S(1)} fusion(bf16[4,4,240,512]{3,2,1,0:T(8,128)(2,1)} %get-tuple-element.7, f32[512]{0:T(512)S(1)} %copy-done.18, f32[512]{0:T(512)S(1)} %mul.53, f32[512]{0:T(512)S(1)} %sub.70), kind=kLoop, calls=%fused_computation | loop fusion | flops 17694720 | bytes 7870464 | tf_op jit(solution)/shard_map/convert_element_type | solution.py:433
  42.4 1.8 %copy-done.1 = bf16[4,4,240,512]{3,2,1,0:T(8,128)(2,1)} copy-done((bf16[4,4,240,512]{3,2,1,0:T(8,128)(2,1)}, bf16[4,4,240,512]{3,2,1,0:T(8,128)(2,1)S(1)}, u32[]{:S(2)}) %copy-start.1) | copy-done | bytes 3932184
  44.3 3.8 %slice_select_fusion = (bf16[2,4,240,512]{3,2,1,0:T(8,128)(2,1)S(1)}, bf16[2,4,240,512]{3,2,1,0:T(8,128)(2,1)}) fusion(bf16[4,4,240,512]{3,2,1,0:T(8,128)(2,1)} %copy-done.1, pred[]{:T(512)S(6)} %eq.3, bf16[4,240,512]{2,1,0:T(8,128)(2,1)S(1)} %slice_bitcast_fusion), kind=kLoop, calls=%fused_computation.28 | loop fusion | flops 983040 | bytes 8847361 | tf_op jit(solution)/shard_map/jit(_where)/select_n | solution.py:435
  48.1 1.8 %maximum_select_fusion = bf16[4,4,240,512]{3,2,1,0:T(8,128)(2,1)S(1)} fusion(bf16[2,4,240,512]{3,2,1,0:T(8,128)(2,1)} %get-tuple-element.48, bf16[2,4,240,512]{3,2,1,0:T(8,128)(2,1)S(1)} %get-tuple-element.47, pred[4]{0:T(512)(128)(4,1)S(1)} %compare_and_fusion), kind=kLoop, calls=%fused_computation.1 | loop fusion | flops 3932160 | bytes 7864324 | tf_op jit(solution)/shard_map/jit(_where)/select_n | solution.py:439
  49.9 4.8 %pad_slice_fusion.1 = (bf16[2,2,240,512]{3,2,1,0:T(8,128)(2,1)S(1)}, bf16[2,2,240,512]{3,2,1,0:T(8,128)(2,1)S(1)}, bf16[2,2,240,512]{3,2,1,0:T(8,128)(2,1)S(1)},...) fusion(bf16[4,4,240,512]{3,2,1,0:T(8,128)(2,1)S(1)} %maximum_se, ...), kind=kLoop, calls=%fused_computation.55 | loop fusion | bytes 14745600 | tf_op jit(solution)/shard_map/slice | solution.py:384
  54.7 2.1 %fusion.19 = (bf16[2,2,240,512]{3,2,1,0:T(8,128)(2,1)S(1)}, bf16[2,2,240,512]{3,2,1,0:T(8,128)(2,1)S(1)}, bf16[2,2,240,512]{3,2,1,0:T(8,128)(2,1)}, bf16[2,2,240...) fusion(bf16[4,4,240,512]{3,2,1,0:T(8,128)(2,1)S(1)} %maximum_select_fusion), kind=kLoop, calls=%fused_computation.73 | loop fusion | bytes 14745600 | tf_op jit(solution)/shard_map/slice | solution.py:384
  56.8 5.2 %pad_maximum_fusion = (bf16[2,2,240,1536]{3,2,1,0:T(8,128)(2,1)}, bf16[2,2,240,1536]{3,2,1,0:T(8,128)(2,1)}) fusion(bf16[2,2,240,512]{3,2,1,0:T(8,128)(2,1)S(1)} %get-tuple-element.21, bf16[2,2,240,512]{3,2,1,0:T(8,128)(2,1)} %get-tuple-element.45, bf16[2,2,240,512]{3,2,1,0:T(8,128)(2,1)} %get-tuple-element.46, ...), kind=kLoop, calls=%fused_computation.6 | loop fusion | flops 17694720 | bytes 11796480 | tf_op jit(solution)/shard_map/concatenate | solution.py:383
  62.0 1.4 slice-done.2
  64.0 5.3 %fusion.18 = (bf16[1,1,3,512,512]{4,3,2,1,0:T(8,128)(2,1)S(1)}, bf16[1,1,3,512,512]{4,3,2,1,0:T(8,128)(2,1)}, bf16[1,1,3,512,512]{4,3,2,1,0:T(8,128)(2,1)}, bf16...) fusion(bf16[3,3,3,512,512]{4,3,2,1,0:T(8,128)(2,1)S(1)} %bitcast.68), kind=kLoop, calls=%fused_computation.72 | loop fusion | bytes 28311552 | tf_op jit(solution)/shard_map/slice | solution.py:388
  69.3 4.1 %fusion.21 = f32[960,512]{1,0:T(8,128)S(1)} fusion(bf16[960,1536]{1,0:T(8,128)(2,1)} %bitcast.74, bf16[1536,512]{1,0:T(8,128)(2,1)} %bitcast.88), kind=kOutput, calls=%fused_computation.75 | convolution fusion | flops 1509949440 | bytes 6488064 | tf_op jit(solution)/shard_map/dot_general | solution.py:386
  73.5 1.7 fusion.20
  75.7 1.0 copy-done.12
  76.7 1.7 fusion.22
  78.4 1.7 fusion.23
  80.1 4.8 %pad_slice_fusion = (bf16[2,2,240,512]{3,2,1,0:T(8,128)(2,1)S(1)}, bf16[2,2,240,512]{3,2,1,0:T(8,128)(2,1)S(1)}, bf16[2,2,240,512]{3,2,1,0:T(8,128)(2,1)S(1)}, b...) fusion(bf16[4,4,240,512]{3,2,1,0:T(8,128)(2,1)S(1)} %maximum_se, ...), kind=kLoop, calls=%fused_computation.54 | loop fusion | bytes 17694720 | tf_op jit(solution)/shard_map/slice | solution.py:384
  85.7 0.8 copy-done.10
  86.5 1.7 fusion.24
  88.2 1.7 fusion.25
  89.9 0.8 pad_maximum_fusion.6
  91.3 1.7 fusion.26
  93.0 1.7 fusion.27
  94.7 2.1 %add_add_fusion = f32[960,512]{1,0:T(8,128)S(1)} fusion(f32[960,512]{1,0:T(8,128)S(1)} %fusion.27, f32[960,512]{1,0:T(8,128)S(1)} %fusion.26, f32[960,512]{1,0:T(8,128)S(1)} %fusion.25, f32[960,512]{1,0:T(8,128)S(1)} %fusion.24, f32[960,512]{1,0:T(8,128)S(1)} %fusion.23, f32[960,512]{1,0:T(8,128)S(1)} %fusion.22, f32[960,512]{1,0:T(8,128)S(1)} %fusion.20, ...), kind=kOutput, calls=%fused_computation.29 | convolution fusion | flops 1513881600 | bytes 22216704 | tf_op jit(solution)/shard_map/dot_general | solution.py:386
  98.8 8.8 %stats.1 = f32[32,1,128]{2,1,0:T(1,128)} custom-call(f32[1,1,128]{2,1,0:T(1,128)} %fusion.16.stat_ref), custom_call_target="tpu_custom_call" | custom-call | tf_op jit(solution)/shard_map/stats/pallas_call | solution.py:445
  107.6 0.8 slice.216
  108.4 0.7 slice_reduce_fusion
  110.2 1.3 fusion.9
  111.5 64.8 %attend.1 = bf16[2,480,512]{2,1,0:T(8,128)(2,1)} custom-call(bf16[2,480,512]{2,1,0:T(8,128)(2,1)} %bitcast.72, bf16[512,512]{1,0:T(8,128)(2,1)} %wq_ref.1, bf16[512,512]{1,0:T(8,128)(2,1)} %wk_ref.1, bf16[512,512]{1,0:T(8,128)(2,1)} %wv_ref.1), custom_call_target="tpu_custom_call" | custom-call | tf_op jit(solution)/shard_map/attend/pallas_call | solution.py:458
  176.3 2.8 %fusion.4 = bf16[2,2,240,512]{3,2,1,0:T(8,128)(2,1)} fusion(bf16[2,2,240,512]{3,2,1,0:T(8,128)(2,1)S(1)} %get-tuple-element.10, bf16[2,2,240,512]{3,2,1,0:T(8,128)(2,1)} %bitcast.89, f32[512]{0:T(512)S(1)} %copy-done.19, bf16[512,512]{1,0:T(8,128)(2,1)S(1)} %copy-done), kind=kOutput, calls=%fused_computation.22 | convolution fusion | flops 505282560 | bytes 3475456 | tf_op jit(solution)/shard_map/dot_general | solution.py:482
  (85 shorter events, 7.8 us)
Async XLA Ops:
  0.0 176.3 %copy-start = (bf16[512,512]{1,0:T(8,128)(2,1)S(1)}, bf16[512,512]{1,0:T(8,128)(2,1)}, u32[]{:S(2)}) copy-start(bf16[512,512]{1,0:T(8,128)(2,1)} %param.22) | copy-start | bytes 1572868
  0.0 38.2 %copy-start.16 = (f32[512]{0:T(512)S(1)}, f32[512]{0:T(512)}, u32[]{:S(2)}) copy-start(f32[512]{0:T(512)} %param.13) | copy-start | bytes 6148
  0.0 38.4 %copy-start.18 = (f32[512]{0:T(512)S(1)}, f32[512]{0:T(512)}, u32[]{:S(2)}) copy-start(f32[512]{0:T(512)} %param.14) | copy-start | bytes 6148
  42.4 1.9 %copy-start.1 = (bf16[4,4,240,512]{3,2,1,0:T(8,128)(2,1)}, bf16[4,4,240,512]{3,2,1,0:T(8,128)(2,1)S(1)}, u32[]{:S(2)}) copy-start(bf16[4,4,240,512]{3,2,1,0:T(8,128)(2,1)S(1)} %multiply_convert_fusion) | copy-start | bytes 11796484
  54.7 7.3 %slice-start = ((s8[14155776]{0:T(1024)(128)(4,1)}), s8[4194304]{0:T(1024)(128)(4,1)S(1)}, s32[]{:S(2)}) async-start(s8[14155776]{0:T(1024)(128)(4,1)} %bitcast.67), calls=%async_computation | async-start | bytes 8388608
  54.7 7.3 %slice-start.1 = ((s8[14155776]{0:T(1024)(128)(4,1)}), s8[4194304]{0:T(1024)(128)(4,1)S(1)}, s32[]{:S(2)}) async-start(s8[14155776]{0:T(1024)(128)(4,1)} %bitcast.67), calls=%async_computation.1 | async-start | bytes 8388608
  54.7 8.8 %slice-start.2 = ((s8[14155776]{0:T(1024)(128)(4,1)}), s8[4194304]{0:T(1024)(128)(4,1)S(1)}, s32[]{:S(2)}) async-start(s8[14155776]{0:T(1024)(128)(4,1)} %bitcast.67), calls=%async_computation.2 | async-start | bytes 8388608
  56.8 7.2 %slice-start.3 = ((s8[14155776]{0:T(1024)(128)(4,1)}), s8[1572864]{0:T(1024)(128)(4,1)S(1)}, s32[]{:S(2)}) async-start(s8[14155776]{0:T(1024)(128)(4,1)} %bitcast.67), calls=%async_computation.3 | async-start | bytes 3145728
  69.3 4.1 %copy-start.6 = (bf16[2,2,240,1536]{3,2,1,0:T(8,128)(2,1)S(1)}, bf16[2,2,240,1536]{3,2,1,0:T(8,128)(2,1)}, u32[]{:S(2)}) copy-start(bf16[2,2,240,1536]{3,2,1,0:T(8,128)(2,1)} %get-tuple-element.53) | copy-start | bytes 8847364
  69.3 4.1 %copy-start.13 = (bf16[1,1,3,512,512]{4,3,2,1,0:T(8,128)(2,1)S(1)}, bf16[1,1,3,512,512]{4,3,2,1,0:T(8,128)(2,1)}, u32[]{:S(2)}) copy-start(bf16[1,1,3,512,512]{4,3,2,1,0:T(8,128)(2,1)} %get-tuple-element.18) | copy-start | bytes 4718596
  73.5 1.7 copy-start.3
  73.5 1.7 copy-start.4
  73.5 1.8 copy-start.5
  75.3 1.4 copy-start.12
  76.7 1.7 copy-start.11
  85.1 1.4 copy-start.10
  86.5 1.7 copy-start.9
  89.9 1.4 copy-start.8
  91.3 1.7 copy-start.7
  94.7 2.1 %copy-start.2 = (bf16[2,2,240,512]{3,2,1,0:T(8,128)(2,1)S(1)}, bf16[2,2,240,512]{3,2,1,0:T(8,128)(2,1)}, u32[]{:S(2)}) copy-start(bf16[2,2,240,512]{3,2,1,0:T(8,128)(2,1)} %feat_ref.1) | copy-start | bytes 2949124
  94.7 2.1 %copy-start.14 = (f32[512]{0:T(512)S(1)}, f32[512]{0:T(512)}, u32[]{:S(2)}) copy-start(f32[512]{0:T(512)} %param.16) | copy-start | bytes 6148
  96.8 13.3 %copy-start.17 = (f32[512]{0:T(512)S(1)}, f32[512]{0:T(512)}, u32[]{:S(2)}) copy-start(f32[512]{0:T(512)} %param.17) | copy-start | bytes 6148
  96.8 13.4 %copy-start.15 = (f32[512]{0:T(512)S(1)}, f32[512]{0:T(512)}, u32[]{:S(2)}) copy-start(f32[512]{0:T(512)} %param.18) | copy-start | bytes 6148
  98.0 78.4 %copy-start.19 = (f32[512]{0:T(512)S(1)}, f32[512]{0:T(512)}, u32[]{:S(2)}) copy-start(f32[512]{0:T(512)} %param.23) | copy-start | bytes 6148

commit v2 on v1

--- a/solution.py
+++ b/solution.py
@@ -29,13 +29,47 @@
     pl.semaphore_wait(barrier, count - 1)
 
 
-def send_stats(count, stripes, me, stat_ref, all_ref, send_sem, recv_sem):
-    all_ref[me] = stat_ref[0]
+def group_total(values):
+    chans = values.shape[-1]
+    each = chans // GROUPS
+    lane = lax.broadcasted_iota(jnp.int32, values.shape, 1)
+    step = 1
+    while step < each:
+        ahead = pltpu.roll(values, chans - step, 1)
+        behind = pltpu.roll(values, step, 1)
+        values = values + jnp.where((lane // step) % 2 == 0, ahead, behind)
+        step *= 2
+    return values
+
+
+def rows_of_8(line):
+    return jnp.broadcast_to(line, (8, line.shape[-1]))
+
+
+def is_mean_lane(shape):
+    each = shape[-1] // GROUPS
+    return lax.broadcasted_iota(jnp.int32, shape, 1) % each < each // 2
+
+
+def share_stats(count, stripes, me, blocks, all_ref, send_sem, recv_sem):
+    first = blocks[0]()
+    chans = first.shape[-1]
+    size = len(blocks) * first.shape[0] * (chans // GROUPS)
+    total = jnp.sum(first, axis=0, keepdims=True)
+    for block in blocks[1:]:
+        total = total + jnp.sum(block(), axis=0, keepdims=True)
+    mean = group_total(rows_of_8(total)) / size
+    spread = jnp.zeros((1, chans), jnp.float32)
+    for block in blocks:
+        gap = block() - mean[:1]
+        spread = spread + jnp.sum(gap * gap, axis=0, keepdims=True)
+    spread = group_total(rows_of_8(spread))
+    all_ref[me] = jnp.where(is_mean_lane(mean.shape), mean, spread)[:1]
 
     def send(step, carry):
         peer = (me + step) % count
         pltpu.make_async_remote_copy(
-            src_ref=stat_ref.at[0],
+            src_ref=all_ref.at[me],
             dst_ref=all_ref.at[me],
             send_sem=send_sem,
             recv_sem=recv_sem,
@@ -45,32 +79,47 @@
         return carry
 
     lax.fori_loop(1, count, send, 0)
-
-
-def wait_stats(count, all_ref, send_sem, recv_sem):
+    return size
+
+
+def norm_terms(count, size, all_ref, send_sem, recv_sem, gain):
     others = all_ref.at[pl.ds(0, count - 1)]
     pltpu.make_async_copy(others, others, recv_sem).wait()
     pltpu.make_async_copy(others, others, send_sem).wait()
-
-
-def stats_kernel(sections, stripes, stat_ref, all_ref, send_sem, recv_sem):
-    count = sections * stripes
-    me = lax.axis_index("tm") * stripes + lax.axis_index("rows")
-    greet_all(count, stripes, me)
-    send_stats(count, stripes, me, stat_ref, all_ref, send_sem, recv_sem)
-    wait_stats(count, all_ref, send_sem, recv_sem)
-
-
-def halo_kernel(
+    stats = all_ref[...]
+    chans = stats.shape[-1]
+    half = chans // GROUPS // 2
+    total = jnp.sum(stats, axis=0)
+    gap = stats - total / count
+    gaps = jnp.sum(gap * gap, axis=0)
+    total = rows_of_8(total)
+    gaps = rows_of_8(gaps)
+    means = is_mean_lane(total.shape)
+    mean = group_total(jnp.where(means, total, 0.0)) / (half * count)
+    spread = group_total(jnp.where(means, gaps * size, total)) / half / (size * count)
+    return mean[:1], (lax.rsqrt(spread + EPS) * gain)[:1]
+
+
+def conv_kernel(
     sections,
     stripes,
-    stat_ref,
     feat_ref,
-    all_ref,
-    ext_ref,
-    send_sem,
-    recv_sem,
-    local_sem,
+    gain1_ref,
+    bias1_ref,
+    weight_ref,
+    bias_ref,
+    gain2_ref,
+    bias2_ref,
+    resid_ref,
+    normed_ref,
+    ext,
+    act,
+    weight,
+    conv,
+    all1,
+    all2,
+    stat_sem,
+    weight_sem,
     out_sem,
     in_sem,
 ):
@@ -78,13 +127,18 @@
     tm = lax.axis_index("tm")
     row = lax.axis_index("rows")
     me = tm * stripes + row
-    frames, high = feat_ref.shape[:2]
-    own = pltpu.make_async_copy(
-        feat_ref, ext_ref.at[pl.ds(frames, frames), pl.ds(1, high)], local_sem
-    )
-    own.start()
+    frames, high, width, chans = feat_ref.shape
+    has_next = tm < sections - 1
+    has_past = tm > 0
+    has_above = row > 0
+    has_below = row < stripes - 1
+
+    loads = [
+        pltpu.make_async_copy(weight_ref.at[a], weight.at[a], weight_sem.at[a]) for a in range(3)
+    ]
+    for load in loads:
+        load.start()
     greet_all(count, stripes, me)
-    send_stats(count, stripes, me, stat_ref, all_ref, send_sem, recv_sem)
 
     def push(src, dst, slot, to_tm, to_row):
         return pltpu.make_async_remote_copy(
@@ -98,19 +152,80 @@
 
     now = pl.ds(frames, frames)
     past = pl.ds(0, frames)
-    down = push(feat_ref.at[:, high - 1], ext_ref.at[now, 0], 0, tm, row + 1)
-    up = push(feat_ref.at[:, 0], ext_ref.at[now, high + 1], 1, tm, row - 1)
-    later = push(feat_ref, ext_ref.at[past, pl.ds(1, high)], 2, tm + 1, row)
-    later_top = push(ext_ref.at[now, 0], ext_ref.at[past, 0], 3, tm + 1, row)
-    later_low = push(ext_ref.at[now, high + 1], ext_ref.at[past, high + 1], 4, tm + 1, row)
-    has_next = tm < sections - 1
-    has_past = tm > 0
-    has_above = row > 0
-    has_below = row < stripes - 1
+    down = push(feat_ref.at[:, high - 1], ext.at[now, 0], 0, tm, row + 1)
+    up = push(feat_ref.at[:, 0], ext.at[now, high + 1], 1, tm, row - 1)
+    later = push(feat_ref, ext.at[past, pl.ds(1, high)], 2, tm + 1, row)
+    later_top = push(ext.at[now, 0], ext.at[past, 0], 3, tm + 1, row)
+    later_low = push(ext.at[now, high + 1], ext.at[past, high + 1], 4, tm + 1, row)
 
     pl.when(has_below)(lambda: down.start())
     pl.when(has_above)(lambda: up.start())
     pl.when(has_next)(lambda: later.start())
+
+    blocks = [
+        lambda f=f, o=o: feat_ref[f, o].astype(jnp.float32)
+        for f in range(frames)
+        for o in range(high)
+    ]
+    size = share_stats(count, stripes, me, blocks, all1, stat_sem.at[0], stat_sem.at[1])
+    mean1, gain1 = norm_terms(count, size, all1, stat_sem.at[0], stat_sem.at[1], gain1_ref[...])
+    bias1 = bias1_ref[...]
+    column = lax.broadcasted_iota(jnp.int32, (width, chans), 0)
+
+    def activate(source, targets):
+        scaled = (source.astype(jnp.float32) - mean1) * gain1 + bias1
+        half = 0.5 * scaled
+        silu = half + half * jnp.tanh(half)
+        before = jnp.where(column == 0, 0.0, pltpu.roll(silu, 1, 0)).astype(jnp.bfloat16)
+        after = jnp.where(column == width - 1, 0.0, pltpu.roll(silu, width - 1, 0)).astype(
+            jnp.bfloat16
+        )
+        here = silu.astype(jnp.bfloat16)
+        for f, r in targets:
+            act[f, r, :, :chans] = before
+            act[f, r, :, chans : 2 * chans] = here
+            act[f, r, :, 2 * chans :] = after
+
+    def open_frames(r):
+        for f in range(frames):
+            act[f, r] = act[frames, r]
+
+    for r in range(1, high + 1):
+        for f in range(frames):
+            activate(feat_ref[f, r - 1], [(frames + f, r)])
+    pl.when(tm == 0)(lambda: [open_frames(r) for r in range(1, high + 1)] and None)
+
+    @pl.when(has_past)
+    def _():
+        later.wait_recv()
+
+        def earlier(index, carry):
+            f = index // high
+            r = 1 + index % high
+            activate(ext[f, r], [(f, r)])
+            return carry
+
+        lax.fori_loop(0, frames * high, earlier, 0)
+
+    cells = frames * width
+
+    def taps(a, r, b):
+        return jnp.dot(
+            act[pl.ds(a, frames), r].reshape(cells, 3 * chans),
+            weight[a, b],
+            preferred_element_type=jnp.float32,
+        ).reshape(frames, width, chans)
+
+    conv[...] = jnp.broadcast_to(bias_ref[...].reshape(1, 1, 1, chans), conv.shape)
+
+    def inner(a, carry):
+        conv[:, 0] += taps(a, 1, 1) + taps(a, 2, 2)
+        conv[:, 1] += taps(a, 1, 0) + taps(a, 2, 1)
+        return carry
+
+    for a in range(3):
+        loads[a].wait()
+    lax.fori_loop(0, 2, inner, 0)
 
     @pl.when(has_above)
     def _():
@@ -122,11 +237,51 @@
         up.wait_recv()
         pl.when(has_next)(lambda: later_low.start())
 
-    @pl.when(has_past)
-    def _():
-        later.wait_recv()
-        pl.when(has_above)(lambda: later_top.wait_recv())
-        pl.when(has_below)(lambda: later_low.wait_recv())
+    lax.fori_loop(2, 3, inner, 0)
+
+    def halo(r, exists, relay):
+        @pl.when(exists)
+        def _():
+            def each(f, carry):
+                activate(ext[frames + f, r], [(frames + f, r)])
+                return carry
+
+            lax.fori_loop(0, frames, each, 0)
+            pl.when(tm == 0)(lambda: open_frames(r))
+
+            @pl.when(has_past)
+            def _():
+                relay.wait_recv()
+
+                def each_past(f, carry):
+                    activate(ext[f, r], [(f, r)])
+                    return carry
+
+                lax.fori_loop(0, frames, each_past, 0)
+
+        @pl.when(jnp.logical_not(exists))
+        def _():
+            act[:, r] = jnp.zeros_like(act[:, r])
+
+    halo(0, has_above, later_top)
+    halo(high + 1, has_below, later_low)
+
+    def outer(a, carry):
+        conv[:, 0] += taps(a, 0, 0)
+        conv[:, 1] += taps(a, high + 1, 2)
+        return carry
+
+    lax.fori_loop(0, 3, outer, 0)
+
+    for f in range(frames):
+        for o in range(high):
+            resid_ref[f, o] = (feat_ref[f, o].astype(jnp.float32) + conv[f, o]).astype(jnp.bfloat16)
+    blocks = [
+        lambda f=f, o=o: resid_ref[f, o].astype(jnp.float32)
+        for f in range(frames)
+        for o in range(high)
+    ]
+    size = share_stats(count, stripes, me, blocks, all2, stat_sem.at[2], stat_sem.at[3])
 
     pl.when(has_below)(lambda: down.wait_send())
     pl.when(has_above)(lambda: up.wait_send())
@@ -137,8 +292,12 @@
         pl.when(has_above)(lambda: later_top.wait_send())
         pl.when(has_below)(lambda: later_low.wait_send())
 
-    own.wait()
-    wait_stats(count, all_ref, send_sem, recv_sem)
+    mean2, gain2 = norm_terms(count, size, all2, stat_sem.at[2], stat_sem.at[3], gain2_ref[...])
+    for f in range(frames):
+        for o in range(high):
+            normed_ref[f, o] = (
+                (resid_ref[f, o].astype(jnp.float32) - mean2) * gain2 + bias2_ref[...]
+            ).astype(jnp.bfloat16)
 
 
 def attend_kernel(
@@ -348,49 +507,6 @@
         pl.when((tm == 0) & has_below)(lambda j=j: across(2 * BAND + j, 8 + j).wait_send())
 
 
-def local_stats(values):
-    chans = values.shape[-1]
-    grouped = values.reshape(-1, GROUPS, chans // GROUPS)
-    size = grouped.shape[0] * grouped.shape[2]
-    mean = jnp.sum(grouped, axis=(0, 2)) / size
-    centered = grouped - mean[:, None]
-    spread = jnp.sum(centered * centered, axis=(0, 2))
-    packed = jnp.concatenate([mean, spread, jnp.zeros((128 - 2 * GROUPS,), jnp.float32)])
-    return packed.reshape(1, 1, 128), size
-
-
-def norm_terms(stats, size, gain, shift):
-    means = stats[:, 0, :GROUPS]
-    spreads = stats[:, 0, GROUPS : 2 * GROUPS]
-    mean = jnp.mean(means, axis=0)
-    gap = means - mean
-    spread = jnp.sum(spreads + size * gap * gap, axis=0) / (size * stats.shape[0])
-    each = gain.shape[0] // GROUPS
-    return jnp.repeat(mean, each), jnp.repeat(lax.rsqrt(spread + EPS), each) * gain, shift
-
-
-def normalize(values, terms):
-    mean, gain, shift = terms
-    return (values - mean) * gain + shift
-
-
-def conv_taps(padded, weight, frames, height, width):
-    chans = padded.shape[-1]
-    total = jnp.zeros((frames * height * width, weight.shape[-1]), jnp.float32)
-    for step_t in range(3):
-        for step_h in range(3):
-            slab = padded[step_t : step_t + frames, step_h : step_h + height]
-            stacked = jnp.concatenate(
-                [slab[:, :, step_w : step_w + width] for step_w in range(3)], axis=-1
-            )
-            total = total + jnp.dot(
-                stacked.reshape(-1, 3 * chans),
-                weight[step_t, step_h].reshape(3 * chans, -1),
-                preferred_element_type=jnp.float32,
-            )
-    return total.reshape(frames, height, width, -1)
-
-
 def shards(
     feat,
     norm1_gain,
@@ -409,51 +525,40 @@
     sections = lax.axis_size("tm")
     stripes = lax.axis_size("rows")
     count = sections * stripes
-    row = lax.axis_index("rows")
     vmem = pl.BlockSpec(memory_space=pltpu.VMEM)
     anywhere = pl.BlockSpec(memory_space=pl.ANY)
-    all_stats = jax.ShapeDtypeStruct((count, 1, 128), jnp.float32)
     dma = pltpu.SemaphoreType.DMA
-
-    stat1, size = local_stats(feat.astype(jnp.float32))
-    stats1, ext = pl.pallas_call(
-        functools.partial(halo_kernel, sections, stripes),
-        out_shape=(
-            all_stats,
-            jax.ShapeDtypeStruct((2 * frames, high + 2, width, chans), jnp.bfloat16),
+    image = jax.ShapeDtypeStruct(feat.shape, jnp.bfloat16)
+    resid, normed = pl.pallas_call(
+        functools.partial(conv_kernel, sections, stripes),
+        out_shape=(image, image),
+        in_specs=[vmem, vmem, vmem, anywhere, vmem, vmem, vmem],
+        out_specs=(vmem, vmem),
+        scratch_shapes=[
+            pltpu.VMEM((2 * frames, high + 2, width, chans), jnp.bfloat16),
+            pltpu.VMEM((2 * frames, high + 2, width, 3 * chans), jnp.bfloat16),
+            pltpu.VMEM((3, 3, 3 * chans, chans), jnp.bfloat16),
+            pltpu.VMEM((frames, high, width, chans), jnp.float32),
+            pltpu.VMEM((count, 1, chans), jnp.float32),
+            pltpu.VMEM((count, 1, chans), jnp.float32),
+            dma((4,)),
+            dma((3,)),
+            dma((5,)),
+            dma((5,)),
+        ],
+        compiler_params=pltpu.CompilerParams(
+            collective_id=0, has_side_effects=True, vmem_limit_bytes=VMEM_LIMIT
         ),
-        in_specs=[vmem, anywhere],
-        out_specs=(vmem, anywhere),
-        scratch_shapes=[dma, dma, dma, dma((5,)), dma((5,))],
-        compiler_params=pltpu.CompilerParams(collective_id=0, has_side_effects=True),
-        name="halo",
-    )(stat1, feat)
-    act = jax.nn.silu(
-        normalize(ext.astype(jnp.float32), norm_terms(stats1, size, norm1_gain, norm1_bias))
-    ).astype(jnp.bfloat16)
-    opening = jnp.broadcast_to(act[frames : frames + 1], act[:frames].shape)
-    past = jnp.where(lax.axis_index("tm") == 0, opening, act[:frames])
-    timed = jnp.concatenate([past, act[frames:]], axis=0)
-    place = row * high - 1 + jnp.arange(high + 2, dtype=jnp.int32)
-    within = (place >= 0) & (place < stripes * high)
-    timed = jnp.where(within[None, :, None, None], timed, jnp.bfloat16(0))
-    padded = jnp.pad(timed, ((0, 0), (0, 0), (1, 1), (0, 0)))
-    conv = conv_taps(padded, conv_weight, frames, high, width) + conv_bias
-    resid = (feat.astype(jnp.float32) + conv).astype(jnp.bfloat16)
-
-    stat2, size = local_stats(resid.astype(jnp.float32))
-    stats2 = pl.pallas_call(
-        functools.partial(stats_kernel, sections, stripes),
-        out_shape=all_stats,
-        in_specs=[vmem],
-        out_specs=vmem,
-        scratch_shapes=[dma, dma],
-        compiler_params=pltpu.CompilerParams(collective_id=1, has_side_effects=True),
-        name="stats",
-    )(stat2)
-    normed = normalize(
-        resid.astype(jnp.float32), norm_terms(stats2, size, norm2_gain, norm2_bias)
-    ).astype(jnp.bfloat16)
+        name="conv",
+    )(
+        feat,
+        norm1_gain[None],
+        norm1_bias[None],
+        conv_weight.reshape(3, 3, 3 * chans, chans),
+        conv_bias[None],
+        norm2_gain[None],
+        norm2_bias[None],
+    )
     cells = high * width
     attn = pl.pallas_call(
         functools.partial(attend_kernel, stripes),

time: 182 us -> 126 us (0.69); the launches traced: 179 us -> 126 us
  other arithmetic: 26.5 us -> 0 us
  local copies, waits for them, and re-layouts: 25.5 us -> 0.01 us
  matrix products: 20.8 us -> 2.82 us
  Pallas kernels: 106 us -> 123 us
    dot_general x9 -> x0, matrix products: 18 us -> none  [conv_taps(): jnp.dot(stacked.reshape(-1, 3 * chans), weight[step_t, step_h].reshape(3...]
    slice x5 -> x0, local copies, waits for them, and re-layouts: 17.8 us -> none  [the longest x3 11.7 us: conv_taps(): slab[:, :, step_w:step_w + width]]
    pallas_call x2 -> x1, Pallas kernels: 41.1 us -> 56.6 us  [shards(): pl.pallas_call(functools.partial(conv_kernel, sections, stripes), out_sha...]
    reduce_sum x12 -> x0, other arithmetic: 7.32 us -> none  [the longest x4 2.11 us: local_stats(): mean = jnp.sum(grouped, axis=(0, 2)) / size]
    concatenate x5 -> x0, other arithmetic: 7.15 us -> none  [conv_taps(): jnp.concatenate([slab[:, :, step_w:step_w + width] for step_w in range(3)...]
    unnamed x48 -> x6, local copies, waits for them, and re-layouts: 6.43 us -> 0.01 us
    select_n x2 -> x0, other arithmetic: 5.55 us -> none  [the longest x1 3.75 us: shards(): past = jnp.where(lax.axis_index('tm') == 0, opening, act[:frames])]
    convert_element_type x2 -> x0, other arithmetic: 5.27 us -> none  [the longest x1 4.02 us: shards(): act = jax.nn.silu(normalize(ext.astype(jnp.float32), norm_terms(stats1, s...]
where the time goes in v2:
time: 126 us
  Pallas kernels  123 us (98%)
  matrix products  2.82 us (2%)
    pallas_call x1, Pallas kernels, shards(): pl.pallas_call(functools.partial(attend_kernel, stripes), out_shape=jax.S...  66 us
    pallas_call x1, Pallas kernels, shards(): pl.pallas_call(functools.partial(conv_kernel, sections, stripes), out_sha...  56.6 us
    dot_general x1, matrix products, shards(): jnp.dot(attn.reshape(-1, chans), w_out, preferred_element_type=jnp.float32)  2.82 us

profile of v2, /device:TPU:9, one launch (start us, length us, event | category | flops | bytes accessed | tf_op | source)
XLA Modules:
  0.0 125.5 jit_solution(9285043161490967501)
XLA Ops:
  0.0 0.0 copy-start
  0.0 56.6 %conv.1 = (bf16[2,2,240,512]{3,2,1,0:T(8,128)(2,1)}, bf16[2,2,240,512]{3,2,1,0:T(8,128)(2,1)}) custom-call(bf16[2,2,240,512]{3,2,1,0:T(8,128)(2,1)} %feat_ref.1, f32[1,512]{1,0:T(1,128)} %bitcast.17, f32[1,512]{1,0:T(1,128)} %bitcast.18, bf16[3,3,1536,512]{3,2,1,0:T(8,128)(2,1)} %bitcast.14, f32[1,512]{1,0:T(1,128)} %bitcast.19, f32[1,512]{1,0:T(1,128)} %bitcast.20, ...), custom_call_target="tpu_custom_call" | custom-call | tf_op jit(solution)/shard_map/conv/pallas_call | solution.py:532
  56.6 0.0 copy-start.1
  56.6 0.0 copy-start.2
  56.7 66.0 %attend.1 = bf16[2,480,512]{2,1,0:T(8,128)(2,1)} custom-call(bf16[2,480,512]{2,1,0:T(8,128)(2,1)} %bitcast.15, bf16[512,512]{1,0:T(8,128)(2,1)} %wq_ref.1, bf16[512,512]{1,0:T(8,128)(2,1)} %wk_ref.1, bf16[512,512]{1,0:T(8,128)(2,1)} %wv_ref.1), custom_call_target="tpu_custom_call" | custom-call | tf_op jit(solution)/shard_map/attend/pallas_call | solution.py:563
  122.7 0.0 copy-done
  122.7 0.0 copy-done.1
  122.7 0.0 copy-done.2
  122.7 2.8 %add_convert_fusion = bf16[2,2,240,512]{3,2,1,0:T(8,128)(2,1)} fusion(bf16[2,2,240,512]{3,2,1,0:T(8,128)(2,1)S(1)} %copy-done.1, bf16[2,2,240,512]{3,2,1,0:T(8,128)(2,1)} %bitcast.16, f32[512]{0:T(512)S(1)} %copy-done.2, bf16[512,512]{1,0:T(8,128)(2,1)S(1)} %copy-done), kind=kOutput, calls=%fused_computation | convolution fusion | flops 505282560 | bytes 3475456 | tf_op jit(solution)/shard_map/dot_general | solution.py:587
Async XLA Ops:
  0.0 122.7 %copy-start = (bf16[512,512]{1,0:T(8,128)(2,1)S(1)}, bf16[512,512]{1,0:T(8,128)(2,1)}, u32[]{:S(2)}) copy-start(bf16[512,512]{1,0:T(8,128)(2,1)} %param.22) | copy-start | bytes 1572868
  56.6 66.0 %copy-start.1 = (bf16[2,2,240,512]{3,2,1,0:T(8,128)(2,1)S(1)}, bf16[2,2,240,512]{3,2,1,0:T(8,128)(2,1)}, u32[]{:S(2)}) copy-start(bf16[2,2,240,512]{3,2,1,0:T(8,128)(2,1)} %get-tuple-element.7) | copy-start | bytes 2949124
  56.6 66.0 %copy-start.2 = (f32[512]{0:T(512)S(1)}, f32[512]{0:T(512)}, u32[]{:S(2)}) copy-start(f32[512]{0:T(512)} %param.23) | copy-start | bytes 6148

commit v3 on v2

--- a/solution.py
+++ b/solution.py
@@ -100,7 +100,7 @@
     return mean[:1], (lax.rsqrt(spread + EPS) * gain)[:1]
 
 
-def conv_kernel(
+def block_kernel(
     sections,
     stripes,
     feat_ref,
@@ -110,18 +110,33 @@
     bias_ref,
     gain2_ref,
     bias2_ref,
+    wq_ref,
+    wk_ref,
+    wv_ref,
     resid_ref,
-    normed_ref,
+    attn_ref,
     ext,
     act,
     weight,
     conv,
     all1,
     all2,
+    window,
+    query,
+    key,
+    value,
+    top,
+    total,
+    mixed,
+    reply,
     stat_sem,
     weight_sem,
     out_sem,
     in_sem,
+    window_out,
+    window_in,
+    back_out,
+    back_in,
 ):
     count = sections * stripes
     tm = lax.axis_index("tm")
@@ -275,79 +290,18 @@
 
     for f in range(frames):
         for o in range(high):
-            resid_ref[f, o] = (feat_ref[f, o].astype(jnp.float32) + conv[f, o]).astype(jnp.bfloat16)
-    blocks = [
-        lambda f=f, o=o: resid_ref[f, o].astype(jnp.float32)
-        for f in range(frames)
-        for o in range(high)
-    ]
-    size = share_stats(count, stripes, me, blocks, all2, stat_sem.at[2], stat_sem.at[3])
-
-    pl.when(has_below)(lambda: down.wait_send())
-    pl.when(has_above)(lambda: up.wait_send())
-
-    @pl.when(has_next)
-    def _():
-        later.wait_send()
-        pl.when(has_above)(lambda: later_top.wait_send())
-        pl.when(has_below)(lambda: later_low.wait_send())
-
-    mean2, gain2 = norm_terms(count, size, all2, stat_sem.at[2], stat_sem.at[3], gain2_ref[...])
-    for f in range(frames):
-        for o in range(high):
-            normed_ref[f, o] = (
-                (resid_ref[f, o].astype(jnp.float32) - mean2) * gain2 + bias2_ref[...]
+            resid_ref[f, pl.ds(o * width, width)] = (
+                feat_ref[f, o].astype(jnp.float32) + conv[f, o]
             ).astype(jnp.bfloat16)
 
-
-def attend_kernel(
-    stripes,
-    normed_ref,
-    wq_ref,
-    wk_ref,
-    wv_ref,
-    out_ref,
-    window,
-    query,
-    key,
-    value,
-    top,
-    total,
-    mixed,
-    reply,
-    in_sem,
-    out_sem,
-    back_in,
-    back_out,
-):
-    bands = stripes // BAND
-    tm = lax.axis_index("tm")
-    row = lax.axis_index("rows")
-    band = row // BAND
     k = row % BAND
-    first = band * BAND
-    cells, chans = normed_ref.shape[1:]
+    first = row - k
+    half = k // 2
+    has_band_above = first > 0
+    has_band_below = first + BAND < stripes
     scale = 1.0 / math.sqrt(chans)
-    has_above = band > 0
-    has_below = band < bands - 1
-    half = k // 2
-
-    barrier = pltpu.get_barrier_semaphore()
-
-    def greet(to_tm, to_row):
-        pl.semaphore_signal(barrier, inc=1, device_id=(to_tm, to_row), device_id_type=MESH)
-
-    greet(1 - tm, row)
-    pl.when(has_above)(lambda: greet(tm, row - BAND))
-    pl.when(has_below)(lambda: greet(tm, row + BAND))
-    for j in range(2):
-        pl.when(2 * tm + j != k)(lambda j=j: greet(half, first + 2 * tm + j))
-    peers = 1 + has_above.astype(jnp.int32) + has_below.astype(jnp.int32)
-    for j in range(2):
-        peers = peers + (2 * tm + j != k).astype(jnp.int32)
-    pl.semaphore_wait(barrier, peers)
-
-    def push(src, dst, sent, got, to_tm, to_row):
+
+    def send(src, dst, sent, got, to_tm, to_row):
         return pltpu.make_async_remote_copy(
             src_ref=src,
             dst_ref=dst,
@@ -358,11 +312,11 @@
         )
 
     def scatter(j):
-        return push(
-            normed_ref.at[j],
+        return send(
+            resid_ref.at[j],
             window.at[BAND + k],
-            out_sem.at[j],
-            in_sem.at[BAND + k],
+            window_out.at[j],
+            window_in.at[BAND + k],
             half,
             first + 2 * tm + j,
         )
@@ -373,127 +327,156 @@
         @pl.when(2 * tm + j == k)
         def _(j=j):
             pltpu.make_async_copy(
-                normed_ref.at[j], window.at[BAND + k], in_sem.at[BAND + k]
+                resid_ref.at[j], window.at[BAND + k], window_in.at[BAND + k]
             ).start()
 
+    blocks = [
+        lambda f=f, o=o: resid_ref[f, pl.ds(o * width, width)].astype(jnp.float32)
+        for f in range(frames)
+        for o in range(high)
+    ]
+    size = share_stats(count, stripes, me, blocks, all2, stat_sem.at[2], stat_sem.at[3])
+
+    pl.when(has_below)(lambda: down.wait_send())
+    pl.when(has_above)(lambda: up.wait_send())
+
+    @pl.when(has_next)
+    def _():
+        later.wait_send()
+        pl.when(has_above)(lambda: later_top.wait_send())
+        pl.when(has_below)(lambda: later_low.wait_send())
+
+    mean2, gain2 = norm_terms(count, size, all2, stat_sem.at[2], stat_sem.at[3], gain2_ref[...])
+    bias2 = bias2_ref[...]
+
     def arrived(slot):
-        pltpu.make_async_copy(window.at[slot], window.at[slot], in_sem.at[slot]).wait()
+        pltpu.make_async_copy(window.at[slot], window.at[slot], window_in.at[slot]).wait()
 
     def across(slot, number):
-        return push(
+        return send(
             window.at[slot],
             window.at[slot],
-            out_sem.at[number],
-            in_sem.at[slot],
+            window_out.at[number],
+            window_in.at[slot],
             1 - tm,
             row,
         )
 
     def downward(slot, number):
-        return push(
+        return send(
             window.at[slot],
             window.at[slot - BAND],
-            out_sem.at[number],
-            in_sem.at[slot - BAND],
+            window_out.at[number],
+            window_in.at[slot - BAND],
             tm,
             row + BAND,
         )
 
     def upward(slot, number):
-        return push(
+        return send(
             window.at[slot],
             window.at[slot + BAND],
-            out_sem.at[number],
-            in_sem.at[slot + BAND],
+            window_out.at[number],
+            window_in.at[slot + BAND],
             tm,
             row - BAND,
         )
 
-    def update(q, slot):
-        scores = (
-            lax.dot_general(
-                query[q], key[...], (((1,), (1,)), ((), ())), preferred_element_type=jnp.float32
+    def normed(slot):
+        return ((window[slot].astype(jnp.float32) - mean2) * gain2 + bias2).astype(jnp.bfloat16)
+
+    def against(left, right):
+        return lax.dot_general(
+            left, right, (((1,), (1,)), ((), ())), preferred_element_type=jnp.float32
+        )
+
+    def queries(t, carry):
+        i = (t + k) % 2
+        slot = BAND + 2 * tm + i
+        arrived(slot)
+        pl.when(has_band_below)(lambda: downward(slot, 2 + i).start())
+        pl.when(has_band_above)(lambda: upward(slot, 4 + i).start())
+        across(slot, 6 + i).start()
+        query[i] = jnp.dot(normed(slot), wq_ref[...], preferred_element_type=jnp.float32).astype(
+            jnp.bfloat16
+        )
+        return carry
+
+    lax.fori_loop(0, 2, queries, 0)
+    top[...] = jnp.full_like(top, -1e30)
+    total[...] = jnp.zeros_like(total)
+    mixed[...] = jnp.zeros_like(mixed)
+
+    def update(wanted):
+        scores = [against(key[...], query[q]) for q in wanted]
+        for q, score in zip(wanted, scores):
+            old = top[q]
+            new = jnp.maximum(old, jnp.max(score, axis=0, keepdims=True))
+            expo = jnp.exp((score - new) * scale)
+            shrink = jnp.exp((old - new) * scale)
+            total[q] = total[q] * shrink + jnp.sum(expo, axis=0, keepdims=True)
+            top[q] = new
+            mixed[q] = mixed[q] * shrink + jnp.dot(
+                value[...], expo.astype(jnp.bfloat16), preferred_element_type=jnp.float32
             )
-            * scale
-        )
-        old = top[q]
-        new = jnp.maximum(old, jnp.max(scores, axis=-1, keepdims=True))
-        expo = jnp.exp(scores - new[:, :1])
-        shrink = jnp.exp(old - new)
-        total[q] = total[q] * shrink + jnp.sum(expo, axis=-1, keepdims=True)
-        top[q] = new
-        mixed[q] = mixed[q] * shrink[:, :1] + jnp.dot(
-            expo.astype(jnp.bfloat16), value[...], preferred_element_type=jnp.float32
-        )
-
-    def queries(t, carry):
-        slot = BAND + 2 * tm + t
-        arrived(slot)
-        pl.when(has_below)(lambda: downward(slot, 2 + t).start())
-        pl.when(has_above)(lambda: upward(slot, 4 + t).start())
-        across(slot, 6 + t).start()
-        query[t] = jnp.dot(window[slot], wq_ref[...], preferred_element_type=jnp.float32).astype(
-            jnp.bfloat16
-        )
-        top[t] = jnp.full_like(top[t], -1e30)
-        total[t] = jnp.zeros_like(total[t])
-        mixed[t] = jnp.zeros_like(mixed[t])
-        return carry
-
-    lax.fori_loop(0, 2, queries, 0)
 
     def slots(t, carry):
-        stage = t // 2
-        i = t % 2
+        paired = (t >= 4) & (t < 8)
+        stage = jnp.where(paired, 2 + t % 2, jnp.where(t < 4, t // 2, 4))
+        i = (jnp.where(paired, (t - 4) // 2, t % 2) + k) % 2
         slot = i + jnp.where(
             stage == 0,
             BAND + 2 * tm,
             jnp.where(
                 stage == 1,
                 BAND + 2 * (1 - tm),
-                jnp.where(stage == 2, 2 * tm, jnp.where(stage == 3, 2 * BAND + 2 * tm, 2 + 6 * tm)),
+                jnp.where(
+                    stage == 2,
+                    jnp.where(tm == 1, 2, 2 * BAND),
+                    jnp.where(stage == 3, jnp.where(tm == 1, 2 * BAND + 2, 0), 2 + 6 * tm),
+                ),
             ),
         )
-        inside = ((slot >= BAND) | has_above) & ((slot < 2 * BAND) | has_below)
+        inside = ((slot >= BAND) | has_band_above) & ((slot < 2 * BAND) | has_band_below)
 
         @pl.when(inside)
         def _():
             pl.when(stage > 0)(lambda: arrived(slot))
-            pl.when((stage == 2) & (tm == 1))(lambda: across(slot, 8 + i).start())
-            pl.when((stage == 3) & (tm == 0))(lambda: across(slot, 8 + i).start())
+            pl.when(stage == 2)(lambda: across(slot, 8 + i).start())
+            cells_here = normed(slot)
             key[...] = jnp.dot(
-                window[slot], wk_ref[...], preferred_element_type=jnp.float32
+                cells_here, wk_ref[...], preferred_element_type=jnp.float32
             ).astype(jnp.bfloat16)
-            value[...] = jnp.dot(
-                window[slot], wv_ref[...], preferred_element_type=jnp.float32
-            ).astype(jnp.bfloat16)
-
-            def one(q, inner):
-                start = 2 * tm + q
-                pl.when((slot >= start) & (slot <= start + 2 * BAND))(lambda: update(q, slot))
-                return inner
-
-            lax.fori_loop(0, 2, one, 0)
+            value[...] = against(wv_ref[...], cells_here).astype(jnp.bfloat16)
+            offset = slot - 2 * tm
+            pl.when((offset >= 1) & (offset <= 2 * BAND))(lambda: update((0, 1)))
+            pl.when(offset == 0)(lambda: update((0,)))
+            pl.when(offset == 2 * BAND + 1)(lambda: update((1,)))
 
         return carry
 
     lax.fori_loop(0, 10, slots, 0)
 
     def answer(q):
-        return push(
-            reply.at[q], out_ref.at[k % 2], back_out.at[q], back_in.at[k % 2], half, first + 2 * tm + q
+        return send(
+            reply.at[q],
+            attn_ref.at[k % 2],
+            back_out.at[q],
+            back_in.at[k % 2],
+            half,
+            first + 2 * tm + q,
         )
 
     for q in range(2):
-        reply[q] = (mixed[q] / total[q][:, :1]).astype(jnp.bfloat16)
+        reply[q] = jnp.transpose(mixed[q] / total[q]).astype(jnp.bfloat16)
         pl.when(2 * tm + q != k)(lambda q=q: answer(q).start())
 
         @pl.when(2 * tm + q == k)
         def _(q=q):
-            pltpu.make_async_copy(reply.at[q], out_ref.at[k % 2], back_in.at[k % 2]).start()
+            pltpu.make_async_copy(reply.at[q], attn_ref.at[k % 2], back_in.at[k % 2]).start()
 
     for j in range(2):
-        pltpu.make_async_copy(out_ref.at[j], out_ref.at[j], back_in.at[j]).wait()
+        pltpu.make_async_copy(attn_ref.at[j], attn_ref.at[j], back_in.at[j]).wait()
 
         @pl.when(2 * tm + j != k)
         def _(j=j):
@@ -501,10 +484,10 @@
             answer(j).wait_send()
 
         across(BAND + 2 * tm + j, 6 + j).wait_send()
-        pl.when(has_below)(lambda j=j: downward(BAND + 2 * tm + j, 2 + j).wait_send())
-        pl.when(has_above)(lambda j=j: upward(BAND + 2 * tm + j, 4 + j).wait_send())
-        pl.when((tm == 1) & has_above)(lambda j=j: across(2 + j, 8 + j).wait_send())
-        pl.when((tm == 0) & has_below)(lambda j=j: across(2 * BAND + j, 8 + j).wait_send())
+        pl.when(has_band_below)(lambda j=j: downward(BAND + 2 * tm + j, 2 + j).wait_send())
+        pl.when(has_band_above)(lambda j=j: upward(BAND + 2 * tm + j, 4 + j).wait_send())
+        pl.when((tm == 1) & has_band_above)(lambda j=j: across(2 + j, 8 + j).wait_send())
+        pl.when((tm == 0) & has_band_below)(lambda j=j: across(2 * BAND + j, 8 + j).wait_send())
 
 
 def shards(
@@ -528,11 +511,12 @@
     vmem = pl.BlockSpec(memory_space=pltpu.VMEM)
     anywhere = pl.BlockSpec(memory_space=pl.ANY)
     dma = pltpu.SemaphoreType.DMA
-    image = jax.ShapeDtypeStruct(feat.shape, jnp.bfloat16)
-    resid, normed = pl.pallas_call(
-        functools.partial(conv_kernel, sections, stripes),
+    cells = high * width
+    image = jax.ShapeDtypeStruct((frames, cells, chans), jnp.bfloat16)
+    resid, attn = pl.pallas_call(
+        functools.partial(block_kernel, sections, stripes),
         out_shape=(image, image),
-        in_specs=[vmem, vmem, vmem, anywhere, vmem, vmem, vmem],
+        in_specs=[vmem, vmem, vmem, anywhere] + [vmem] * 6,
         out_specs=(vmem, vmem),
         scratch_shapes=[
             pltpu.VMEM((2 * frames, high + 2, width, chans), jnp.bfloat16),
@@ -541,15 +525,27 @@
             pltpu.VMEM((frames, high, width, chans), jnp.float32),
             pltpu.VMEM((count, 1, chans), jnp.float32),
             pltpu.VMEM((count, 1, chans), jnp.float32),
+            pltpu.VMEM((3 * BAND, cells, chans), jnp.bfloat16),
+            pltpu.VMEM((2, cells, chans), jnp.bfloat16),
+            pltpu.VMEM((cells, chans), jnp.bfloat16),
+            pltpu.VMEM((chans, cells), jnp.bfloat16),
+            pltpu.VMEM((2, 1, cells), jnp.float32),
+            pltpu.VMEM((2, 1, cells), jnp.float32),
+            pltpu.VMEM((2, chans, cells), jnp.float32),
+            pltpu.VMEM((2, cells, chans), jnp.bfloat16),
             dma((4,)),
             dma((3,)),
             dma((5,)),
             dma((5,)),
+            dma((10,)),
+            dma((3 * BAND,)),
+            dma((2,)),
+            dma((2,)),
         ],
         compiler_params=pltpu.CompilerParams(
             collective_id=0, has_side_effects=True, vmem_limit_bytes=VMEM_LIMIT
         ),
-        name="conv",
+        name="block",
     )(
         feat,
         norm1_gain[None],
@@ -558,36 +554,15 @@
         conv_bias[None],
         norm2_gain[None],
         norm2_bias[None],
+        w_query,
+        w_key,
+        w_value.T,
     )
-    cells = high * width
-    attn = pl.pallas_call(
-        functools.partial(attend_kernel, stripes),
-        out_shape=jax.ShapeDtypeStruct((frames, cells, chans), jnp.bfloat16),
-        in_specs=[vmem] * 4,
-        out_specs=vmem,
-        scratch_shapes=[
-            pltpu.VMEM((3 * BAND, cells, chans), jnp.bfloat16),
-            pltpu.VMEM((2, cells, chans), jnp.bfloat16),
-            pltpu.VMEM((cells, chans), jnp.bfloat16),
-            pltpu.VMEM((cells, chans), jnp.bfloat16),
-            pltpu.VMEM((2, cells, 128), jnp.float32),
-            pltpu.VMEM((2, cells, 128), jnp.float32),
-            pltpu.VMEM((2, cells, chans), jnp.float32),
-            pltpu.VMEM((2, cells, chans), jnp.bfloat16),
-            dma((3 * BAND,)),
-            dma((10,)),
-            dma((2,)),
-            dma((2,)),
-        ],
-        compiler_params=pltpu.CompilerParams(
-            collective_id=2, has_side_effects=True, vmem_limit_bytes=VMEM_LIMIT
-        ),
-        name="attend",
-    )(normed.reshape(frames, cells, chans), w_query, w_key, w_value)
     output = jnp.dot(
         attn.reshape(-1, chans), w_out, preferred_element_type=jnp.float32
     ).reshape(frames, high, width, chans)
-    return (resid.astype(jnp.float32) + out_bias + output).astype(jnp.bfloat16)
+    resid = resid.reshape(feat.shape).astype(jnp.float32)
+    return (resid + out_bias + output).astype(jnp.bfloat16)
 
 
 def solution(mesh):

time: 126 us -> 115 us (0.913)
  Pallas kernels: 123 us -> 110 us
  local copies, waits for them, and re-layouts: 0.01 us -> 2.11 us
    pallas_call x2 -> x1, Pallas kernels: 123 us -> 110 us  [shards(): pl.pallas_call(functools.partial(block_kernel, sections, stripes), out_sh...]
    unnamed x6 -> x5, local copies, waits for them, and re-layouts: 0.01 us -> 2.11 us
where the time goes in v3:
time: 115 us
  Pallas kernels  110 us (96%)
  matrix products  3.12 us (3%)
  local copies, waits for them, and re-layouts  2.11 us (2%)
    pallas_call x1, Pallas kernels, shards(): pl.pallas_call(functools.partial(block_kernel, sections, stripes), out_sh...  110 us
    dot_general x1, matrix products, shards(): jnp.dot(attn.reshape(-1, chans), w_out, preferred_element_type=jnp.float32)  3.12 us

profile of v3, /device:TPU:9, one launch (start us, length us, event | category | flops | bytes accessed | tf_op | source)
XLA Modules:
  0.0 115.1 jit_solution(36427887097347245)
XLA Ops:
  0.0 0.0 copy-start
  0.0 2.1 %copy.13 = bf16[512,512]{0,1:T(8,128)(2,1)} copy(bf16[512,512]{1,0:T(8,128)(2,1)} %param.21) | data formatting | bytes 1048576 | tf_op args[9]
  2.1 0.0 copy-start.1
  2.1 109.8 %block.1 = (bf16[2,480,512]{2,1,0:T(8,128)(2,1)}, bf16[2,480,512]{2,1,0:T(8,128)(2,1)}) custom-call(bf16[2,2,240,512]{3,2,1,0:T(8,128)(2,1)} %feat_ref.1, f32[1,512]{1,0:T(1,128)} %bitcast.18, f32[1,512]{1,0:T(1,128)} %bitcast.19, bf16[3,3,1536,512]{3,2,1,0:T(8,128)(2,1)} %bitcast.16, f32[1,512]{1,0:T(1,128)} %bitcast.20, f32[1,512]{1,0:T(1,128)} %bitcast.21, ...), custom_call_target="tpu_custom_call" | custom-call | tf_op jit(solution)/shard_map/block/pallas_call | solution.py:516
  112.0 0.0 copy-done
  112.0 0.0 copy-done.1
  112.0 3.1 %fusion.1 = bf16[2,2,240,512]{3,2,1,0:T(8,128)(2,1)} fusion(bf16[2,2,240,512]{3,2,1,0:T(8,128)(2,1)} %bitcast.23, bf16[2,2,240,512]{3,2,1,0:T(8,128)(2,1)} %bitcast.24, f32[512]{0:T(512)S(1)} %copy-done.1, bf16[512,512]{1,0:T(8,128)(2,1)S(1)} %copy-done), kind=kOutput, calls=%fused_computation.2 | convolution fusion | flops 505282560 | bytes 3475456 | tf_op jit(solution)/shard_map/dot_general | solution.py:561
Async XLA Ops:
  0.0 112.0 %copy-start = (bf16[512,512]{1,0:T(8,128)(2,1)S(1)}, bf16[512,512]{1,0:T(8,128)(2,1)}, u32[]{:S(2)}) copy-start(bf16[512,512]{1,0:T(8,128)(2,1)} %param.22) | copy-start | bytes 1572868
  2.1 109.9 %copy-start.1 = (f32[512]{0:T(512)S(1)}, f32[512]{0:T(512)}, u32[]{:S(2)}) copy-start(f32[512]{0:T(512)} %param.23) | copy-start | bytes 6148

commit v4 on v3

--- a/solution.py
+++ b/solution.py
@@ -129,6 +129,7 @@
     total,
     mixed,
     reply,
+    value_weight,
     stat_sem,
     weight_sem,
     out_sem,
@@ -165,16 +166,26 @@
             device_id_type=MESH,
         )
 
-    now = pl.ds(frames, frames)
     past = pl.ds(0, frames)
-    down = push(feat_ref.at[:, high - 1], ext.at[now, 0], 0, tm, row + 1)
-    up = push(feat_ref.at[:, 0], ext.at[now, high + 1], 1, tm, row - 1)
-    later = push(feat_ref, ext.at[past, pl.ds(1, high)], 2, tm + 1, row)
-    later_top = push(ext.at[now, 0], ext.at[past, 0], 3, tm + 1, row)
-    later_low = push(ext.at[now, high + 1], ext.at[past, high + 1], 4, tm + 1, row)
-
-    pl.when(has_below)(lambda: down.start())
-    pl.when(has_above)(lambda: up.start())
+    low = high + 1
+    later = push(feat_ref, ext.at[past, pl.ds(1, high)], 0, tm + 1, row)
+    down = []
+    up = []
+    top_on = []
+    low_on = []
+    for f in range(frames):
+        n = 1 + 4 * f
+        own = frames + f
+        down.append(push(feat_ref.at[f, high - 1], ext.at[own, 0], n, tm, row + 1))
+        up.append(push(feat_ref.at[f, 0], ext.at[own, low], n + 1, tm, row - 1))
+        top_on.append(push(ext.at[own, 0], ext.at[f, 0], n + 2, tm + 1, row))
+        low_on.append(push(ext.at[own, low], ext.at[f, low], n + 3, tm + 1, row))
+
+    def send_edges(f):
+        pl.when(has_below)(lambda: down[f].start())
+        pl.when(has_above)(lambda: up[f].start())
+
+    send_edges(0)
     pl.when(has_next)(lambda: later.start())
 
     blocks = [
@@ -183,6 +194,9 @@
         for o in range(high)
     ]
     size = share_stats(count, stripes, me, blocks, all1, stat_sem.at[0], stat_sem.at[1])
+    for f in range(1, frames):
+        send_edges(f)
+    value_weight[...] = jnp.transpose(wv_ref[...])
     mean1, gain1 = norm_terms(count, size, all1, stat_sem.at[0], stat_sem.at[1], gain1_ref[...])
     bias1 = bias1_ref[...]
     column = lax.broadcasted_iota(jnp.int32, (width, chans), 0)
@@ -240,55 +254,65 @@
 
     for a in range(3):
         loads[a].wait()
+    def pass_on(f):
+        @pl.when(has_next & has_above)
+        def _():
+            down[f].wait_recv()
+            top_on[f].start()
+
+        @pl.when(has_next & has_below)
+        def _():
+            up[f].wait_recv()
+            low_on[f].start()
+
     lax.fori_loop(0, 2, inner, 0)
-
-    @pl.when(has_above)
-    def _():
-        down.wait_recv()
-        pl.when(has_next)(lambda: later_top.start())
-
-    @pl.when(has_below)
-    def _():
-        up.wait_recv()
-        pl.when(has_next)(lambda: later_low.start())
-
+    pass_on(0)
     lax.fori_loop(2, 3, inner, 0)
-
-    def halo(r, exists, relay):
+    pass_on(1)
+
+    def tap(e, r, f):
+        o, b = (0, 0) if r == 0 else (high - 1, 2)
+        conv[f, o] += jnp.dot(act[e, r], weight[e - f, b], preferred_element_type=jnp.float32)
+
+    edges = ((0, has_above, down, top_on), (low, has_below, up, low_on))
+
+    def first_edges(r, exists, near, relay):
         @pl.when(exists)
         def _():
-            def each(f, carry):
-                activate(ext[frames + f, r], [(frames + f, r)])
-                return carry
-
-            lax.fori_loop(0, frames, each, 0)
-            pl.when(tm == 0)(lambda: open_frames(r))
+            pl.when(has_past)(lambda: near[0].wait_recv())
+            activate(ext[2, r], [(2, r)])
+            tap(2, r, 0)
+            tap(2, r, 1)
+
+            @pl.when(tm == 0)
+            def _():
+                act[0, r] = act[2, r]
+                act[1, r] = act[2, r]
+                tap(1, r, 0)
+                tap(1, r, 1)
 
             @pl.when(has_past)
             def _():
-                relay.wait_recv()
-
-                def each_past(f, carry):
-                    activate(ext[f, r], [(f, r)])
-                    return carry
-
-                lax.fori_loop(0, frames, each_past, 0)
-
-        @pl.when(jnp.logical_not(exists))
+                relay[0].wait_recv()
+                activate(ext[0, r], [(0, r)])
+
+            tap(0, r, 0)
+
+    def last_edges(r, exists, near, relay):
+        @pl.when(exists)
         def _():
-            act[:, r] = jnp.zeros_like(act[:, r])
-
-    halo(0, has_above, later_top)
-    halo(high + 1, has_below, later_low)
-
-    def outer(a, carry):
-        conv[:, 0] += taps(a, 0, 0)
-        conv[:, 1] += taps(a, high + 1, 2)
-        return carry
-
-    lax.fori_loop(0, 3, outer, 0)
-
-    for f in range(frames):
+            pl.when(has_past)(lambda: near[1].wait_recv())
+            activate(ext[3, r], [(3, r)])
+            tap(3, r, 1)
+
+            @pl.when(has_past)
+            def _():
+                relay[1].wait_recv()
+                activate(ext[1, r], [(1, r)])
+                tap(1, r, 0)
+                tap(1, r, 1)
+
+    def settle(f):
         for o in range(high):
             resid_ref[f, pl.ds(o * width, width)] = (
                 feat_ref[f, o].astype(jnp.float32) + conv[f, o]
@@ -321,14 +345,23 @@
             first + 2 * tm + j,
         )
 
-    for j in range(2):
-        pl.when(2 * tm + j != k)(lambda j=j: scatter(j).start())
+    def leave(j):
+        settle(j)
+        pl.when(2 * tm + j != k)(lambda: scatter(j).start())
 
         @pl.when(2 * tm + j == k)
-        def _(j=j):
+        def _():
             pltpu.make_async_copy(
                 resid_ref.at[j], window.at[BAND + k], window_in.at[BAND + k]
             ).start()
+
+    for edge in edges:
+        first_edges(*edge)
+    pl.when(tm == 0)(lambda: leave(0))
+    for edge in edges:
+        last_edges(*edge)
+    pl.when(has_past)(lambda: leave(0))
+    leave(1)
 
     blocks = [
         lambda f=f, o=o: resid_ref[f, pl.ds(o * width, width)].astype(jnp.float32)
@@ -337,14 +370,12 @@
     ]
     size = share_stats(count, stripes, me, blocks, all2, stat_sem.at[2], stat_sem.at[3])
 
-    pl.when(has_below)(lambda: down.wait_send())
-    pl.when(has_above)(lambda: up.wait_send())
-
-    @pl.when(has_next)
-    def _():
-        later.wait_send()
-        pl.when(has_above)(lambda: later_top.wait_send())
-        pl.when(has_below)(lambda: later_low.wait_send())
+    for f in range(frames):
+        pl.when(has_below)(lambda f=f: down[f].wait_send())
+        pl.when(has_above)(lambda f=f: up[f].wait_send())
+        pl.when(has_next & has_above)(lambda f=f: top_on[f].wait_send())
+        pl.when(has_next & has_below)(lambda f=f: low_on[f].wait_send())
+    pl.when(has_next)(lambda: later.wait_send())
 
     mean2, gain2 = norm_terms(count, size, all2, stat_sem.at[2], stat_sem.at[3], gain2_ref[...])
     bias2 = bias2_ref[...]
@@ -447,7 +478,7 @@
             key[...] = jnp.dot(
                 cells_here, wk_ref[...], preferred_element_type=jnp.float32
             ).astype(jnp.bfloat16)
-            value[...] = against(wv_ref[...], cells_here).astype(jnp.bfloat16)
+            value[...] = against(value_weight[...], cells_here).astype(jnp.bfloat16)
             offset = slot - 2 * tm
             pl.when((offset >= 1) & (offset <= 2 * BAND))(lambda: update((0, 1)))
             pl.when(offset == 0)(lambda: update((0,)))
@@ -533,10 +564,11 @@
             pltpu.VMEM((2, 1, cells), jnp.float32),
             pltpu.VMEM((2, chans, cells), jnp.float32),
             pltpu.VMEM((2, cells, chans), jnp.bfloat16),
+            pltpu.VMEM((chans, chans), jnp.bfloat16),
             dma((4,)),
             dma((3,)),
-            dma((5,)),
-            dma((5,)),
+            dma((9,)),
+            dma((9,)),
             dma((10,)),
             dma((3 * BAND,)),
             dma((2,)),
@@ -556,7 +588,7 @@
         norm2_bias[None],
         w_query,
         w_key,
-        w_value.T,
+        w_value,
     )
     output = jnp.dot(
         attn.reshape(-1, chans), w_out, preferred_element_type=jnp.float32

time: 115 us -> 108 us (0.939)
  Pallas kernels: 110 us -> 105 us
  local copies, waits for them, and re-layouts: 2.11 us -> 0.01 us
    pallas_call x1, Pallas kernels: 110 us -> 105 us  [shards(): pl.pallas_call(functools.partial(block_kernel, sections, stripes), out_sh...]
    unnamed x5 -> x4, local copies, waits for them, and re-layouts: 2.11 us -> 0.01 us
where the time goes in v4:
time: 108 us
  Pallas kernels  105 us (97%)
  matrix products  3.12 us (3%)
    pallas_call x1, Pallas kernels, shards(): pl.pallas_call(functools.partial(block_kernel, sections, stripes), out_sh...  105 us
    dot_general x1, matrix products, shards(): jnp.dot(attn.reshape(-1, chans), w_out, preferred_element_type=jnp.float32)  3.12 us

profile of v4, /device:TPU:9, one launch (start us, length us, event | category | flops | bytes accessed | tf_op | source)
XLA Modules:
  0.0 107.9 jit_solution(15692610814533164974)
XLA Ops:
  0.0 0.0 copy-start
  0.0 0.0 copy-start.1
  0.0 104.7 %block.1 = (bf16[2,480,512]{2,1,0:T(8,128)(2,1)}, bf16[2,480,512]{2,1,0:T(8,128)(2,1)}) custom-call(bf16[2,2,240,512]{3,2,1,0:T(8,128)(2,1)} %feat_ref.1, f32[1,512]{1,0:T(1,128)} %bitcast.16, f32[1,512]{1,0:T(1,128)} %bitcast.17, bf16[3,3,1536,512]{3,2,1,0:T(8,128)(2,1)} %bitcast.15, f32[1,512]{1,0:T(1,128)} %bitcast.18, f32[1,512]{1,0:T(1,128)} %bitcast.19, ...), custom_call_target="tpu_custom_call" | custom-call | tf_op jit(solution)/shard_map/block/pallas_call | solution.py:547
  104.8 0.0 copy-done
  104.8 0.0 copy-done.1
  104.8 3.1 %fusion.1 = bf16[2,2,240,512]{3,2,1,0:T(8,128)(2,1)} fusion(bf16[2,2,240,512]{3,2,1,0:T(8,128)(2,1)} %bitcast.21, bf16[2,2,240,512]{3,2,1,0:T(8,128)(2,1)} %bitcast.22, f32[512]{0:T(512)S(1)} %copy-done.1, bf16[512,512]{1,0:T(8,128)(2,1)S(1)} %copy-done), kind=kOutput, calls=%fused_computation.2 | convolution fusion | flops 505282560 | bytes 3475456 | tf_op jit(solution)/shard_map/dot_general | solution.py:593
Async XLA Ops:
  0.0 104.8 %copy-start = (bf16[512,512]{1,0:T(8,128)(2,1)S(1)}, bf16[512,512]{1,0:T(8,128)(2,1)}, u32[]{:S(2)}) copy-start(bf16[512,512]{1,0:T(8,128)(2,1)} %param.22) | copy-start | bytes 1572868
  0.0 104.8 %copy-start.1 = (f32[512]{0:T(512)S(1)}, f32[512]{0:T(512)}, u32[]{:S(2)}) copy-start(f32[512]{0:T(512)} %param.23) | copy-start | bytes 6148
